TPU v7x, 1024 devices: a whole 4x4x32 slice. The times are simulated.
1024 devices in a mesh: node: 128 (over x, z), feat: 8 (over y, core).
Axes of the slice: x: 4, y: 4, z: 32, core: 2. Of those that a mesh axis runs over, the one named last changes fastest.
Arguments:
- features: bfloat16 [256, 524288], P('feat', 'node'), may hold values from -6 to 6
- weight_one: bfloat16 [256, 256], replicated, may hold values from -0.375 to 0.375
- weight_two: bfloat16 [256, 256], replicated, may hold values from -0.375 to 0.375
- blk_rows: int32 [128, 128], P('node'), may hold values from 0 to 31, as said below
- blk_cols: int32 [128, 128], P('node'), may hold values from 0 to 4095, as said below
- blk_counts: int32 [128], P('node'), may hold values from 32 to 128, as said below
- adj_values: bfloat16 [16384, 128, 128], P('node')
- adj_tvalues: bfloat16 [16384, 128, 128], P('node'), as said below
- cotangent: bfloat16 [256, 524288], P('feat', 'node'), may hold values from -0.0078125 to 0.0078125
Outputs:
- hidden_out: bfloat16 [256, 524288], P('feat', 'node')
- grad_one: float32 [256, 256], replicated
- grad_two: float32 [256, 256], replicated
Inputs may be any that keep to these rules, and one draw needn't show every extreme that they name: `blk_rows`: slots m >= blk_counts[s] of shard s are unused and hold 0. `blk_cols`: for shard s a live slot's block column lies in shards s - 1, s or s + 1; no (row, column) block repeats among a shard's live slots; the set of live blocks of the whole matrix is symmetric; at most 16 live slots of a shard have their column in shard s + 1, and at most 16 in shard s - 1, and some shard reaches this bound on each side; unused slots hold s * 32. `blk_counts`: every shard's 32 diagonal blocks are live; some shard uses all 128 slots. `adj_tvalues`: each live slot holds the transpose of the adj_values block at the mirrored block position, so B is the transpose of A.
All inputs are finite; a program needn't handle non-finite values.
Results may differ from a plain program's by a relative error of at most 0.015.
Values may be sent and summed in bfloat16 or wider, within the bound.
No kernel may reach another device: no remote copies, remote signals or barrier semaphores. Data moves between devices by JAX's collectives and lax.ppermute only.
A program may use at most 64 MiB of HBM per device.

v0:
```python
import jax
import jax.numpy as jnp
from jax import lax
from jax.sharding import PartitionSpec as P

BLK = 128
NBD = 32


def padded(block, sides, width):
    for axis, dim in sides:
        count = lax.axis_size(axis)
        forward = [(i, i + 1) for i in range(count - 1)]
        backward = [(target, source) for source, target in forward]
        low = lax.ppermute(
            lax.slice_in_dim(block, block.shape[dim] - width, None, axis=dim), axis, forward
        )
        high = lax.ppermute(lax.slice_in_dim(block, 0, width, axis=dim), axis, backward)
        block = jnp.concatenate([low, block, high], axis=dim)
    return block


def silu_grad(values):
    sigma = jax.nn.sigmoid(values)
    return sigma * (1.0 + values * (1.0 - sigma))


def to_rows(source):
    return lax.all_to_all(source, "feat", split_axis=1, concat_axis=0, tiled=True)


def to_feats(source):
    return lax.all_to_all(source, "feat", split_axis=0, concat_axis=1, tiled=True)


def rank_among(sort_key, member):
    earlier = member[None, :] & (sort_key[None, :] < sort_key[:, None])
    return jnp.sum(earlier.astype(jnp.int32), axis=1)


def slot_tables(block_rows, block_cols, live_total, position):
    half = NBD // 2
    slot_ids = jnp.arange(block_rows.shape[0])
    slot_live = slot_ids < live_total
    own_start = position * NBD
    local_col = block_cols - own_start + NBD
    to_right = slot_live & (block_cols >= own_start + NBD)
    to_left = slot_live & (block_cols < own_start)
    send_key = block_rows * (4 * NBD) + local_col
    recv_key = local_col * (4 * NBD) + block_rows
    send_right = rank_among(send_key, to_right)
    send_left = rank_among(send_key, to_left)
    recv_right = rank_among(recv_key, to_right)
    recv_left = rank_among(recv_key, to_left)
    row_hit = block_rows[:, None] == jnp.arange(NBD)[None, :]
    place = jnp.arange(half)[None, :]
    high_hit = (to_right[:, None] & (send_right[:, None] == place)).astype(jnp.float32)
    low_hit = (to_left[:, None] & (send_left[:, None] == place)).astype(jnp.float32)
    high_pick = jnp.einsum("mr,mk->rk", row_hit.astype(jnp.float32), high_hit).astype(jnp.bfloat16)
    low_pick = jnp.einsum("mr,mk->rk", row_hit.astype(jnp.float32), low_hit).astype(jnp.bfloat16)
    compact_cols = jnp.where(
        to_right,
        half + NBD + recv_right,
        jnp.where(to_left, recv_left, half + block_cols - own_start),
    )
    targets = jnp.where(slot_live, block_rows, NBD)
    return {
        "local": local_col,
        "compact": compact_cols,
        "high": high_pick,
        "low": low_pick,
        "targets": targets,
    }


def extend(source, tables):
    breadth, extent = source.shape
    extended = padded(source, (("node", 1),), extent)
    return (extended, tables["local"])


def apply_blocks(source, tables, adj_blocks):
    breadth, extent = source.shape
    extended, columns = extend(source, tables)
    grouped = extended.reshape(breadth, -1, BLK)
    picked = jnp.take(grouped, columns, axis=1)
    partial_value = jnp.einsum(
        "fmk,mjk->mfj", picked, adj_blocks, preferred_element_type=jnp.float32
    )
    summed = jax.ops.segment_sum(partial_value, tables["targets"], num_segments=NBD)
    return jnp.transpose(summed, (1, 0, 2)).reshape(breadth, extent)


def transform(source, weight):
    spread = to_rows(source)
    product = to_feats(
        jnp.einsum("io,in->on", weight, spread, preferred_element_type=jnp.float32).astype(
            jnp.bfloat16
        )
    )
    return (spread, product)


def shards(
    features,
    weight_one,
    weight_two,
    blk_rows,
    blk_cols,
    blk_counts,
    adj_values,
    adj_tvalues,
    cotangent,
):
    position = lax.axis_index("node")
    tables = slot_tables(blk_rows.reshape(-1), blk_cols.reshape(-1), blk_counts[0], position)
    input_rows, proj_one = transform(features, weight_one)
    pre_one = apply_blocks(proj_one, tables, adj_values)
    hidden_one = jax.nn.silu(pre_one).astype(jnp.bfloat16)
    hidden_rows, proj_two = transform(hidden_one, weight_two)
    pre_two = apply_blocks(proj_two, tables, adj_values)
    hidden_out = jax.nn.silu(pre_two).astype(jnp.bfloat16)
    delta_two = (cotangent.astype(jnp.float32) * silu_grad(pre_two)).astype(jnp.bfloat16)
    back_two = apply_blocks(delta_two, tables, adj_tvalues).astype(jnp.bfloat16)
    back_two_rows = to_rows(back_two)
    partial_two = jnp.einsum(
        "in,on->io", hidden_rows, back_two_rows, preferred_element_type=jnp.float32
    )
    grad_two = partial_two
    carry_rows = jnp.einsum(
        "io,on->in", weight_two, back_two_rows, preferred_element_type=jnp.float32
    ).astype(jnp.bfloat16)
    carry_one = to_feats(carry_rows)
    delta_one = (carry_one.astype(jnp.float32) * silu_grad(pre_one)).astype(jnp.bfloat16)
    back_one = apply_blocks(delta_one, tables, adj_tvalues).astype(jnp.bfloat16)
    back_one_rows = to_rows(back_one)
    partial_one = jnp.einsum(
        "in,on->io", input_rows, back_one_rows, preferred_element_type=jnp.float32
    )
    grad_one, grad_two = lax.psum((partial_one, grad_two), ("node", "feat"))
    return (hidden_out, grad_one, grad_two)


def solution(mesh):
    return jax.shard_map(
        shards,
        mesh=mesh,
        in_specs=(
            P("feat", "node"),
            P(),
            P(),
            P("node", None),
            P("node", None),
            P("node"),
            P("node", None, None),
            P("node", None, None),
            P("feat", "node"),
        ),
        out_specs=(P("feat", "node"), P(), P()),
        check_vma=False,
    )
```

profile of v0, /device:TPU:1, one launch (start us, length us, event | category | flops | bytes accessed | tf_op | source)
XLA Modules:
  0.0 1094.6 jit_solution(17746394638805891201)
XLA Ops:
  8.2 23.1 %all_to_all.118 = bf16[32,8,512]{2,0,1:T(8,128)(2,1)S(1)} all-to-all(bf16[32,8,512]{2,0,1:T(8,128)(2,1)S(1)} %bitcast.168), channel_id=1, replica_groups=mesh['node'=128,'feat'=8] {'feat'}, dimensions={1} | all-to-all | bytes 524288 | tf_op jit(solution)/shard_map/all_to_all | solution.py:29
  31.3 1.9 convolution_convert_fusion.2
  33.1 4.4 all-to-all-start.1
  38.2 5.8 all-to-all-done.1
  45.3 4.0 collective-permute-start
  49.8 2.9 collective-permute-done.1
  55.4 4.8 fusion.6
  60.3 5.9 scatter_fusion
  66.8 11.1 %all_to_all.119 = bf16[32,8,512]{2,0,1:T(8,128)(2,1)S(1)} all-to-all(bf16[32,8,512]{2,0,1:T(8,128)(2,1)S(1)} %copy.48), channel_id=1, replica_groups=mesh['node'=128,'feat'=8] {'feat'}, dimensions={1} | all-to-all | bytes 524288 | tf_op jit(solution)/shard_map/all_to_all | solution.py:29
  78.2 9.9 all_to_all.120
  89.5 4.7 collective-permute-start.2
  94.6 3.2 collective-permute-done.3
  100.5 4.8 fusion.4
  105.4 5.9 scatter_fusion.1
  111.3 1.9 fusion.30
  113.2 4.0 collective-permute-start.4
  118.5 2.3 collective-permute-done.4
  120.8 3.8 collective-permute-done.5
  126.4 4.8 fusion.2
  131.3 5.9 scatter_fusion.2
  137.6 12.1 %all_to_all.121 = bf16[32,8,512]{2,0,1:T(8,128)(2,1)S(1)} all-to-all(bf16[32,8,512]{2,0,1:T(8,128)(2,1)S(1)} %copy.57), channel_id=1, replica_groups=mesh['node'=128,'feat'=8] {'feat'}, dimensions={1} | all-to-all | bytes 524288 | tf_op jit(solution)/shard_map/all_to_all | solution.py:29
  149.9 10.0 all_to_all.122
  160.2 3.2 collective-permute-start.6
  164.7 3.2 collective-permute-done.6
  167.9 3.8 collective-permute-done.7
  172.7 4.5 fusion
  177.3 5.9 scatter_fusion.3
  184.3 5.6 all-to-all-start.6
  190.8 5.5 all-to-all-done.6
  197.3 887.0 %all-reduce.3.cloned.1.call-done = (f32[256,256]{0,1:T(8,128)}, f32[256,256]{1,0:T(8,128)}) async-done(((f32[256,256]{0,1:T(8,128)}, f32[256,256]{1,0:T(8,128)}), (f32[256,256]{0,1:T(8,128)}, f32[256,256]{1,0:T(8,128)})) %all-reduce.3.cloned.1.call-update) | async-done | bytes 524304 | tf_op jit(solution)/shard_map/psum | solution.py:140
  1084.3 1.8 copy.63
  1086.1 1.7 copy.94
  (69 shorter events, 20.2 us)
Async XLA Ops:
  7.2 70.8 %copy-start = (bf16[256,256]{1,0:T(8,128)(2,1)S(1)}, bf16[256,256]{1,0:T(8,128)(2,1)}, u32[]{:S(2)}) copy-start(bf16[256,256]{1,0:T(8,128)(2,1)} %param.13) | copy-start | bytes 393220
  7.2 31.0 %copy-start.5 = (s32[1,128]{1,0:T(1,128)S(1)}, s32[1,128]{1,0:T(1,128)}, u32[]{:S(2)}) copy-start(s32[1,128]{1,0:T(1,128)} %param.15) | copy-start | bytes 1540
  7.2 38.1 %copy-start.6 = (s32[1,128]{1,0:T(1,128)S(1)}, s32[1,128]{1,0:T(1,128)}, u32[]{:S(2)}) copy-start(s32[1,128]{1,0:T(1,128)} %param.14) | copy-start | bytes 1540
  33.1 10.9 all-to-all-start.1
  44.0 8.7 collective-permute-start.1
  45.3 8.3 collective-permute-start
  78.0 20.7 %copy-start.1 = (bf16[32,8,512]{2,0,1:T(8,128)(2,1)}, bf16[32,8,512]{2,0,1:T(8,128)(2,1)S(1)}, u32[]{:S(2)}) copy-start(bf16[32,8,512]{2,0,1:T(8,128)(2,1)S(1)} %all_to_all.119) | copy-start | bytes 786436
  88.2 9.6 collective-permute-start.3
  89.5 9.2 collective-permute-start.2
  113.2 7.6 collective-permute-start.4
  117.2 7.4 collective-permute-start.5
  149.7 10.5 copy-start.3
  160.2 7.8 collective-permute-start.6
  163.4 8.4 collective-permute-start.7
  183.1 6.7 copy-start.2
  183.2 6.7 copy-start.4
  184.3 12.1 %all-to-all-start.6 = ((bf16[32,8,512]{2,0,1:T(8,128)(2,1)}), bf16[32,8,512]{2,0,1:T(8,128)(2,1)S(1)}, u32[]{:S(2)}, u32[]{:S(2)}) async-start(bf16[32,8,512]{2,0,1:T(8,128)(2,1)} %copy.62), calls=%async_computation.6 | async-start | bytes 524288 | tf_op jit(solution)/shard_map/all_to_all | solution.py:29
  189.8 894.5 %all-reduce.3.cloned.1.call-start = ((), (), s32[]{:S(2)}) async-start(), calls=%async_computation.7 | async-start | bytes 1048576 | tf_op jit(solution)/shard_map/psum | solution.py:140
Sparse Core Ops, SparseCore 0:
  197.5 886.8 all-reduce.2
where the time goes:
time: 1100 us; the launch traced here: 1090 us
  waiting for transfers between devices  919 us (84%)
  blocking collectives  66.2 us (6%)
  starting transfers between devices  31 us (3%)
  other arithmetic  26.2 us (2%)
  matrix products  23.3 us (2%)
  between operations  15.1 us (1%)
  local copies, waits for them, and re-layouts  13.4 us (1%)
    psum x1, waiting for transfers between devices, shards(): grad_one, grad_two = lax.psum((partial_one, grad_two), ('node', 'feat'))  887 us
    all_to_all x3, blocking collectives, to_rows(): lax.all_to_all(source, 'feat', split_axis=1, concat_axis=0, tiled=True)  46.3 us
    scatter-add x4, other arithmetic, apply_blocks(): jax.ops.segment_sum(partial_value, tables['targets'], num_segments=NBD)  23.4 us
  transfers between devices with their start and end apart: 11, of which 11 were waited for; matrix products, arithmetic and copies ran while one was open for 0% of the time, Pallas kernels for 0%

commit v1 on v0

v1 whole, which is shorter than its diff:
```python
import jax
import jax.numpy as jnp
import numpy as np
from jax import lax
from jax.experimental import pallas as pl
from jax.experimental.pallas import tpu as pltpu
from jax.sharding import Mesh, PartitionSpec as P

BLK = 128
NBD = 32
HALO = 16
GROUPS = 8
PER_GROUP = NBD // GROUPS
FEATS = 32
SLOTS_PER_STEP = 16
BF16 = jnp.bfloat16
F32 = jnp.float32

FINE = {"x": 4, "zhi": 8, "zlo": 4, "y": 4, "core": 2}
NODE = ("x", "zhi", "zlo")
FEAT = ("y", "core")
PLANE = ("x", "y", "core")

SMEM = pl.BlockSpec(memory_space=pltpu.SMEM)
VMEM = pl.BlockSpec(memory_space=pltpu.VMEM)


def blocks_of(dtype=BF16):
    return jax.ShapeDtypeStruct((NBD, FEATS, BLK), dtype)


def halo_blocks():
    return jax.ShapeDtypeStruct((HALO, FEATS, BLK), BF16)


def exchange(array, axes):
    return lax.all_to_all(array, axes, split_axis=0, concat_axis=0, tiled=True)


def halo(send_low, send_high):
    count = lax.axis_size(NODE)
    forward = [(i, i + 1) for i in range(count - 1)]
    backward = [(target, source) for source, target in forward]
    low = lax.ppermute(send_high, NODE, forward)
    high = lax.ppermute(send_low, NODE, backward)
    return low, high


def slot_tables(rows, cols, count, position):
    slot = jnp.arange(rows.shape[0])
    live = slot < count
    local = cols - position * NBD
    side = jnp.where(live & (local < 0), 1, jnp.where(live & (local >= NBD), 2, 0))
    same = side[:, None] == side[None, :]
    send_key = rows * (4 * NBD) + local + NBD
    recv_key = (local + NBD) * (4 * NBD) + rows
    send_rank = jnp.sum(same & (send_key[None, :] < send_key[:, None]), axis=1)
    recv_rank = jnp.sum(same & (recv_key[None, :] < recv_key[:, None]), axis=1)
    place = jnp.where(side > 0, (side - 1) * HALO + send_rank, 4 * HALO)
    hit = place[None, :] == jnp.arange(2 * HALO)[:, None]
    send = jnp.sum(jnp.where(hit, rows[None, :], 0), axis=1)
    own = jnp.where(live, HALO + local, HALO)
    source = jnp.where(side == 1, recv_rank, jnp.where(side == 2, HALO + NBD + recv_rank, own))
    target = jnp.where(live, rows, NBD)
    return send.astype(jnp.int32), source.astype(jnp.int32), target.astype(jnp.int32)


def sigmoid(values):
    return 1.0 / (1.0 + jnp.exp(-values))


def gather_sends(send, blocks, low, high):
    for k in range(HALO):
        low[k] = blocks[send[k]]
        high[k] = blocks[send[HALO + k]]


def split_kernel(send, source, blocks, low, high):
    for b in range(NBD):
        blocks[b] = source[:, b * BLK : (b + 1) * BLK]
    gather_sends(send, blocks, low, high)


def split_blocks(send, source):
    return pl.pallas_call(
        split_kernel,
        in_specs=[SMEM, VMEM],
        out_specs=[VMEM] * 3,
        out_shape=[blocks_of(), halo_blocks(), halo_blocks()],
        name="split_blocks",
    )(send, source)


def sends_kernel(send, blocks, low, high):
    gather_sends(send, blocks, low, high)


def sends_of(send, blocks):
    return pl.pallas_call(
        sends_kernel,
        in_specs=[SMEM, VMEM],
        out_specs=[VMEM] * 2,
        out_shape=[halo_blocks(), halo_blocks()],
        name="sends_of",
    )(send, blocks)


def apply_kernel(source, target, low, own, high, adj, out, held, total):
    step = pl.program_id(0)

    @pl.when(step == 0)
    def _():
        held[0:HALO] = low[...]
        held[HALO : HALO + NBD] = own[...]
        held[HALO + NBD :] = high[...]
        total[...] = jnp.zeros_like(total)

    for j in range(SLOTS_PER_STEP):
        m = step * SLOTS_PER_STEP + j
        part = lax.dot_general(
            held[source[m]], adj[j], (((1,), (1,)), ((), ())), preferred_element_type=F32
        )
        row = target[m]
        total[row] = total[row] + part

    @pl.when(step == pl.num_programs(0) - 1)
    def _():
        out[...] = total[0:NBD].astype(BF16)


def apply_blocks(tables, low, own, high, adj):
    slots = adj.shape[0]
    whole = lambda count: pl.BlockSpec((count, FEATS, BLK), lambda i, *_: (0, 0, 0))
    return pl.pallas_call(
        apply_kernel,
        grid_spec=pltpu.PrefetchScalarGridSpec(
            num_scalar_prefetch=2,
            grid=(slots // SLOTS_PER_STEP,),
            in_specs=[
                whole(HALO),
                whole(NBD),
                whole(HALO),
                pl.BlockSpec((SLOTS_PER_STEP, BLK, BLK), lambda i, *_: (i, 0, 0)),
            ],
            out_specs=whole(NBD),
            scratch_shapes=[
                pltpu.VMEM((2 * HALO + NBD, FEATS, BLK), BF16),
                pltpu.VMEM((NBD + 1, FEATS, BLK), F32),
            ],
        ),
        out_shape=blocks_of(),
        name="apply_blocks",
    )(*tables, low, own, high, adj)


def rows_of(ref):
    parts = []
    for b in range(PER_GROUP):
        parts.append(
            jnp.concatenate([ref[g * PER_GROUP + b] for g in range(GROUPS)], axis=0)
        )
    return jnp.concatenate(parts, axis=1)


def put_rows(ref, values):
    for g in range(GROUPS):
        for b in range(PER_GROUP):
            ref[g * PER_GROUP + b] = values[
                g * FEATS : (g + 1) * FEATS, b * BLK : (b + 1) * BLK
            ]


def mix_one_kernel(spread, weight, hidden, slope):
    pre = lax.dot_general(
        weight[...], rows_of(spread), (((0,), (0,)), ((), ())), preferred_element_type=F32
    )
    sigma = sigmoid(pre)
    put_rows(hidden, (pre * sigma).astype(BF16))
    slope[...] = sigma * (1.0 + pre * (1.0 - sigma))


def mix_one(spread, weight):
    shape = (GROUPS * FEATS, PER_GROUP * BLK)
    return pl.pallas_call(
        mix_one_kernel,
        in_specs=[VMEM] * 2,
        out_specs=[VMEM] * 2,
        out_shape=[blocks_of(), jax.ShapeDtypeStruct(shape, F32)],
        name="mix_one",
    )(spread, weight)


def mix_two_kernel(spread, weight, pre_two):
    pre = lax.dot_general(
        weight[...], rows_of(spread), (((0,), (0,)), ((), ())), preferred_element_type=F32
    )
    put_rows(pre_two, pre.astype(BF16))


def mix_two(spread, weight):
    return pl.pallas_call(
        mix_two_kernel,
        in_specs=[VMEM] * 2,
        out_specs=VMEM,
        out_shape=blocks_of(),
        name="mix_two",
    )(spread, weight)


def turn_kernel(send, pre_two, cotangent, hidden_out, delta, low, high):
    for b in range(NBD):
        span = slice(b * BLK, (b + 1) * BLK)
        pre = pre_two[b].astype(F32)
        sigma = sigmoid(pre)
        hidden_out[:, span] = (pre * sigma).astype(BF16)
        slope = sigma * (1.0 + pre * (1.0 - sigma))
        delta[b] = (cotangent[:, span].astype(F32) * slope).astype(BF16)
    gather_sends(send, delta, low, high)


def turn(send, pre_two, cotangent):
    return pl.pallas_call(
        turn_kernel,
        in_specs=[SMEM, VMEM, VMEM],
        out_specs=[VMEM] * 4,
        out_shape=[
            jax.ShapeDtypeStruct(cotangent.shape, BF16),
            blocks_of(),
            halo_blocks(),
            halo_blocks(),
        ],
        name="turn",
    )(send, pre_two, cotangent)


def grads_kernel(back_two, spread_one, hidden_one, slope, weight, out):
    back = rows_of(back_two)
    along = (((1,), (1,)), ((), ()))
    carry = jnp.dot(weight[...], back, preferred_element_type=F32).astype(BF16)
    delta = (carry.astype(F32) * slope[...]).astype(BF16)
    size = GROUPS * FEATS
    grad_one = lax.dot_general(rows_of(spread_one), delta, along, preferred_element_type=F32)
    grad_two = lax.dot_general(rows_of(hidden_one), back, along, preferred_element_type=F32)
    out[0:size] = grad_one.astype(out.dtype)
    out[size:] = grad_two.astype(out.dtype)


def grads(back_two, spread_one, hidden_one, slope, weight):
    size = GROUPS * FEATS
    return pl.pallas_call(
        grads_kernel,
        in_specs=[VMEM] * 5,
        out_specs=VMEM,
        out_shape=jax.ShapeDtypeStruct((2 * size, size), BF16),
        name="grads",
    )(back_two, spread_one, hidden_one, slope, weight)


def gather_pieces(piece, axes):
    spread = jnp.broadcast_to(piece[None], (lax.axis_size(axes),) + piece.shape)
    return exchange(spread, axes)


def sum_everywhere(partial):
    pieces = exchange(partial.reshape(lax.axis_size(PLANE), -1, BLK), PLANE)
    piece = jnp.sum(pieces.astype(F32), axis=0)
    piece = jnp.sum(gather_pieces(piece, "zlo"), axis=0).astype(BF16)
    piece = jnp.sum(gather_pieces(piece, "zhi").astype(F32), axis=0).astype(BF16)
    return gather_pieces(piece, PLANE).reshape(partial.shape).astype(F32)


def shards(
    features,
    weight_one,
    weight_two,
    blk_rows,
    blk_cols,
    blk_counts,
    adj_values,
    adj_tvalues,
    cotangent,
):
    position = lax.axis_index(NODE)
    send, source, target = slot_tables(
        blk_rows.reshape(-1), blk_cols.reshape(-1), blk_counts[0], position
    )
    tables = (source, target)
    own, low, high = split_blocks(send, features)
    low, high = halo(low, high)
    spread_one = exchange(apply_blocks(tables, low, own, high, adj_values), FEAT)
    hidden_rows, slope_one = mix_one(spread_one, weight_one)
    own = exchange(hidden_rows, FEAT)
    low, high = halo(*sends_of(send, own))
    spread_two = exchange(apply_blocks(tables, low, own, high, adj_values), FEAT)
    pre_two = exchange(mix_two(spread_two, weight_two), FEAT)
    hidden_out, delta_two, low, high = turn(send, pre_two, cotangent)
    low, high = halo(low, high)
    back_two = exchange(apply_blocks(tables, low, delta_two, high, adj_tvalues), FEAT)
    total = sum_everywhere(grads(back_two, spread_one, hidden_rows, slope_one, weight_two))
    size = weight_one.shape[0]
    return (hidden_out, total[:size], total[size:])


def solution(mesh):
    fine = Mesh(np.asarray(mesh.devices).reshape(tuple(FINE.values())), tuple(FINE))
    return jax.shard_map(
        shards,
        mesh=fine,
        in_specs=(
            P(FEAT, NODE),
            P(),
            P(),
            P(NODE, None),
            P(NODE, None),
            P(NODE),
            P(NODE, None, None),
            P(NODE, None, None),
            P(FEAT, NODE),
        ),
        out_specs=(P(FEAT, NODE), P(), P()),
        check_vma=False,
    )
```

time: 1100 us -> 226 us (0.21)
  waiting for transfers between devices: 919 us -> 13.5 us
  blocking collectives: 66.2 us -> 153 us
  Pallas kernels: 0 us -> 36 us
  matrix products: 23.3 us -> 0 us
  other arithmetic: 26.2 us -> 4.65 us
  starting transfers between devices: 31 us -> 11.2 us
  between operations: 15.1 us -> 1.39 us
    psum x1 -> x0, waiting for transfers between devices: 887 us -> none  [shards(): grad_one, grad_two = lax.psum((partial_one, grad_two), ('node', 'feat'))]
    all_to_all x5 -> x9, blocking collectives: 66.2 us -> 153 us  [exchange(): return lax.all_to_all(array, axes, split_axis=0, concat_axis=0, tiled=True)]
    pallas_call x0 -> x9, Pallas kernels: none -> 36 us  [the longest x3 23.6 us: apply_blocks(): pl.pallas_call(apply_kernel, grid_spec=pltpu.PrefetchScalarGridSpec(num_s...]
    scatter-add x4 -> x0, other arithmetic: 23.4 us -> none  [apply_blocks(): jax.ops.segment_sum(partial_value, tables['targets'], num_segments=NBD)]
    dot_general x9 -> x0, matrix products: 23.3 us -> none  [the longest x4 19 us: apply_blocks(): jnp.einsum('fmk,mjk->mfj', picked, adj_blocks, preferred_element_type=jnp...]
    all_to_all x2 -> x0, waiting for transfers between devices: 11.4 us -> none  [the longest x1 5.84 us: to_feats(): lax.all_to_all(source, 'feat', split_axis=0, concat_axis=1, tiled=True)]
  transfers between devices with their start and end apart: 11 -> 6, of which waited for: 11 -> 6; matrix products, arithmetic and copies ran while one was open for 0% -> 0% of each run, Pallas kernels for 0% -> 0%
where the time goes in v1:
time: 226 us; the launch traced here: 224 us
  blocking collectives  153 us (68%)
  Pallas kernels  36 us (16%)
  waiting for transfers between devices  13.5 us (6%)
  starting transfers between devices  11.2 us (5%)
  other arithmetic  4.65 us (2%)
  local copies, waits for them, and re-layouts  4.63 us (2%)
    all_to_all x9, blocking collectives, exchange(): return lax.all_to_all(array, axes, split_axis=0, concat_axis=0, tiled=True)  153 us
    pallas_call x3, Pallas kernels, apply_blocks(): pl.pallas_call(apply_kernel, grid_spec=pltpu.PrefetchScalarGridSpec(num_s...  23.6 us
    ppermute x3, waiting for transfers between devices, halo(): high = lax.ppermute(send_low, NODE, backward)  11.2 us
    ppermute x3, starting transfers between devices, halo(): low = lax.ppermute(send_high, NODE, forward)  7.3 us
  transfers between devices with their start and end apart: 6, of which 6 were waited for; matrix products, arithmetic and copies ran while one was open for 0% of the time, Pallas kernels for 0%

profile of v1, /device:TPU:1, one launch (start us, length us, event | category | flops | bytes accessed | tf_op | source)
XLA Modules:
  0.0 224.1 jit_solution(3878019136794405835)
XLA Ops:
  2.6 1.2 fusion.2
  4.0 1.3 select_reduce_fusion.send
  5.3 1.8 split_blocks.1
  7.1 4.4 %collective-permute-start = (bf16[16,32,128]{2,1,0:T(8,128)(2,1)}, bf16[16,32,128]{2,1,0:T(8,128)(2,1)S(1)}, u32[]{:S(2)}, u32[]{:S(2)}) collective-permute-start(bf16[16,32,128]{2,1,0:T(8,128)(2,1)} %get-tuple-element.14), channel_id=1, source_target_pairs={{0,8},{8,16},{16,24},{24,32},{32,40},{40,48},{48,56},{56,64},{64,7... | collective-permute-start | bytes 393224 | tf_op jit(solution)/shard_map/ppermute | solution.py:44
  11.5 1.3 collective-permute-start.1
  13.7 3.9 %collective-permute-done.1.high = bf16[16,32,128]{2,1,0:T(8,128)(2,1)S(1)} collective-permute-done((bf16[16,32,128]{2,1,0:T(8,128)(2,1)}, bf16[16,32,128]{2,1,0:T(8,128)(2,1)S(1)}, u32[]{:S(2)}, u32[]{:S(2)}) %collective-permute-start.1) | collective-permute-done | bytes 131104 | tf_op jit(solution)/shard_map/ppermute | solution.py:45
  18.2 7.9 %apply_blocks.3 = bf16[32,32,128]{2,1,0:T(8,128)(2,1)} custom-call(s32[128]{0:T(128)} %compare_select_fusion.1.source, s32[128]{0:T(128)} %get-tuple-element.33.target, bf16[16,32,128]{2,1,0:T(8,128)(2,1)} %copy-done, bf16[32,32,128]{2,1,0:T(8,128)(2,1)} %get-tuple-element.15.own, bf16[16,32,128]{2,1,0:T(8,128)(2,1)} %copy-done.1, bf16[128,128,128]{2,1,0:T(8,128)(2,1)} %adj.4), custom_call_target="tpu_custom_call" | custom-call | tf_op jit(solution)/shard_map/apply_blocks/pallas_call | solution.py:134
  26.1 22.6 %all_to_all.45.spread.spread_one = bf16[32,32,128]{2,1,0:T(8,128)(2,1)} all-to-all(bf16[32,32,128]{2,1,0:T(8,128)(2,1)} %apply_blocks.3), channel_id=1, replica_groups=mesh['x'=4,'zhi'=8,'zlo'=4,'y'=4,'core'=2] {'y','core'}, dimensions={0} | all-to-all | bytes 524288 | tf_op jit(solution)/shard_map/all_to_all | solution.py:37
  48.6 2.3 %mix_one.1 = (bf16[32,32,128]{2,1,0:T(8,128)(2,1)}, f32[256,512]{1,0:T(8,128)}) custom-call(bf16[32,32,128]{2,1,0:T(8,128)(2,1)} %all_to_all.45.spread.spread_one, bf16[256,256]{1,0:T(8,128)(2,1)} %weight.3), custom_call_target="tpu_custom_call" | custom-call | tf_op jit(solution)/shard_map/mix_one/pallas_call | solution.py:184
  50.9 11.6 %all_to_all.46.blocks.own = bf16[32,32,128]{2,1,0:T(8,128)(2,1)} all-to-all(bf16[32,32,128]{2,1,0:T(8,128)(2,1)} %get-tuple-element.17.hidden_one), channel_id=1, replica_groups=mesh['x'=4,'zhi'=8,'zlo'=4,'y'=4,'core'=2] {'y','core'}, dimensions={0} | all-to-all | bytes 524288 | tf_op jit(solution)/shard_map/all_to_all | solution.py:37
  62.5 1.7 sends_of.1
  64.1 1.3 collective-permute-start.2
  65.5 1.3 collective-permute-start.3
  66.8 0.9 collective-permute-done.2.low
  67.7 3.7 %collective-permute-done.3.high = bf16[16,32,128]{2,1,0:T(8,128)(2,1)S(1)} collective-permute-done((bf16[16,32,128]{2,1,0:T(8,128)(2,1)}, bf16[16,32,128]{2,1,0:T(8,128)(2,1)S(1)}, u32[]{:S(2)}, u32[]{:S(2)}) %collective-permute-start.3) | collective-permute-done | bytes 131104 | tf_op jit(solution)/shard_map/ppermute | solution.py:45
  72.0 7.9 %apply_blocks.4 = bf16[32,32,128]{2,1,0:T(8,128)(2,1)} custom-call(s32[128]{0:T(128)} %compare_select_fusion.1.source, s32[128]{0:T(128)} %get-tuple-element.33.target, bf16[16,32,128]{2,1,0:T(8,128)(2,1)} %copy-done.3, bf16[32,32,128]{2,1,0:T(8,128)(2,1)} %all_to_all.46.blocks.own, bf16[16,32,128]{2,1,0:T(8,128)(2,1)} %copy-done.5, bf16[128,128,128]{2,1,0:T(8,128)(2,1)} %adj.4), custom_call_target="tpu_custom_call" | custom-call | tf_op jit(solution)/shard_map/apply_blocks/pallas_call | solution.py:134
  79.9 13.0 %all_to_all.47.spread = bf16[32,32,128]{2,1,0:T(8,128)(2,1)} all-to-all(bf16[32,32,128]{2,1,0:T(8,128)(2,1)} %apply_blocks.4), channel_id=1, replica_groups=mesh['x'=4,'zhi'=8,'zlo'=4,'y'=4,'core'=2] {'y','core'}, dimensions={0} | all-to-all | bytes 524288 | tf_op jit(solution)/shard_map/all_to_all | solution.py:37
  92.9 1.9 mix_two.1
  94.8 11.5 %all_to_all.48.pre_two = bf16[32,32,128]{2,1,0:T(8,128)(2,1)} all-to-all(bf16[32,32,128]{2,1,0:T(8,128)(2,1)} %mix_two.1), channel_id=1, replica_groups=mesh['x'=4,'zhi'=8,'zlo'=4,'y'=4,'core'=2] {'y','core'}, dimensions={0} | all-to-all | bytes 524288 | tf_op jit(solution)/shard_map/all_to_all | solution.py:37
  106.4 2.1 turn.1
  108.5 1.6 collective-permute-start.4
  110.2 1.3 collective-permute-start.5
  111.5 0.9 collective-permute-done.4.low
  112.4 3.7 %collective-permute-done.5.high = bf16[16,32,128]{2,1,0:T(8,128)(2,1)S(1)} collective-permute-done((bf16[16,32,128]{2,1,0:T(8,128)(2,1)}, bf16[16,32,128]{2,1,0:T(8,128)(2,1)S(1)}, u32[]{:S(2)}, u32[]{:S(2)}) %collective-permute-start.5) | collective-permute-done | bytes 131104 | tf_op jit(solution)/shard_map/ppermute | solution.py:45
  116.7 7.9 %apply_blocks.5 = bf16[32,32,128]{2,1,0:T(8,128)(2,1)} custom-call(s32[128]{0:T(128)} %compare_select_fusion.1.source, s32[128]{0:T(128)} %get-tuple-element.33.target, bf16[16,32,128]{2,1,0:T(8,128)(2,1)} %copy-done.2, bf16[32,32,128]{2,1,0:T(8,128)(2,1)} %get-tuple-element.22.own, bf16[16,32,128]{2,1,0:T(8,128)(2,1)} %copy-done.4, bf16[128,128,128]{2,1,0:T(8,128)(2,1)} %adj.5), custom_call_target="tpu_custom_call" | custom-call | tf_op jit(solution)/shard_map/apply_blocks/pallas_call | solution.py:134
  124.6 13.0 %all_to_all.49.back_two = bf16[32,32,128]{2,1,0:T(8,128)(2,1)} all-to-all(bf16[32,32,128]{2,1,0:T(8,128)(2,1)} %apply_blocks.5), channel_id=1, replica_groups=mesh['x'=4,'zhi'=8,'zlo'=4,'y'=4,'core'=2] {'y','core'}, dimensions={0} | all-to-all | bytes 524288 | tf_op jit(solution)/shard_map/all_to_all | solution.py:37
  137.6 2.5 %grads.1 = bf16[512,256]{1,0:T(8,128)(2,1)} custom-call(bf16[32,32,128]{2,1,0:T(8,128)(2,1)} %all_to_all.49.back_two, bf16[32,32,128]{2,1,0:T(8,128)(2,1)} %all_to_all.45.spread.spread_one, bf16[32,32,128]{2,1,0:T(8,128)(2,1)} %get-tuple-element.17.hidden_one, f32[256,512]{1,0:T(8,128)} %get-tuple-element.24.slope, bf16[256,256]{1,0:T(8,128)(2,1)} %weight.5), custom_call_target="tpu_custom_call" | custom-call | tf_op jit(solution)/shard_map/grads/pallas_call | solution.py:250
  140.1 1.0 reshape.69
  141.1 22.6 %all_to_all.50 = bf16[32,32,128]{2,1,0:T(8,128)(2,1)S(1)} all-to-all(bf16[32,32,128]{2,1,0:T(8,128)(2,1)S(1)} %reshape.69), channel_id=1, replica_groups=mesh['x'=4,'zhi'=8,'zlo'=4,'y'=4,'core'=2] {'x','y','core'}, dimensions={0} | all-to-all | bytes 524288 | tf_op jit(solution)/shard_map/all_to_all | solution.py:37
  163.8 7.1 %all_to_all.51 = f32[4,32,128]{2,1,0:T(8,128)S(1)} all-to-all(f32[4,32,128]{2,1,0:T(8,128)S(1)} %broadcast_in_dim.66), channel_id=1, replica_groups=mesh['x'=4,'zhi'=8,'zlo'=4,'y'=4,'core'=2] {'zlo'}, dimensions={0} | all-to-all | bytes 131072 | tf_op jit(solution)/shard_map/all_to_all | solution.py:37
  170.9 36.8 %all_to_all.52 = bf16[8,32,128]{2,1,0:T(8,128)(2,1)S(1)} all-to-all(bf16[8,32,128]{2,1,0:T(8,128)(2,1)S(1)} %broadcast_in_dim.67), channel_id=1, replica_groups=mesh['x'=4,'zhi'=8,'zlo'=4,'y'=4,'core'=2] {'zhi'}, dimensions={0} | all-to-all | bytes 131072 | tf_op jit(solution)/shard_map/all_to_all | solution.py:37
  207.8 14.7 %all_to_all.53 = bf16[32,32,128]{2,1,0:T(8,128)(2,1)S(1)} all-to-all(bf16[32,32,128]{2,1,0:T(8,128)(2,1)S(1)} %broadcast_in_dim.68), channel_id=1, replica_groups=mesh['x'=4,'zhi'=8,'zlo'=4,'y'=4,'core'=2] {'x','y','core'}, dimensions={0} | all-to-all | bytes 524288 | tf_op jit(solution)/shard_map/all_to_all | solution.py:37
  (27 shorter events, 6.1 us)
Async XLA Ops:
  7.1 6.6 %collective-permute-start = (bf16[16,32,128]{2,1,0:T(8,128)(2,1)}, bf16[16,32,128]{2,1,0:T(8,128)(2,1)S(1)}, u32[]{:S(2)}, u32[]{:S(2)}) collective-permute-start(bf16[16,32,128]{2,1,0:T(8,128)(2,1)} %get-tuple-element.14), channel_id=1, source_target_pairs={{0,8},{8,16},{16,24},{24,32},{32,40},{40,48},{48,56},{56,64},{64,7... | collective-permute-start | bytes 393224 | tf_op jit(solution)/shard_map/ppermute | solution.py:44
  11.5 6.1 %collective-permute-start.1 = (bf16[16,32,128]{2,1,0:T(8,128)(2,1)}, bf16[16,32,128]{2,1,0:T(8,128)(2,1)S(1)}, u32[]{:S(2)}, u32[]{:S(2)}) collective-permute-start(bf16[16,32,128]{2,1,0:T(8,128)(2,1)} %get-tuple-element.16), channel_id=1, source_target_pairs={{8,0},{16,8},{24,16},{32,24},{40,32},{48,40},{56,48},{64,56},{72,6... | collective-permute-start | bytes 393224 | tf_op jit(solution)/shard_map/ppermute | solution.py:45
  13.7 3.9 %copy-start = (bf16[16,32,128]{2,1,0:T(8,128)(2,1)}, bf16[16,32,128]{2,1,0:T(8,128)(2,1)S(1)}, u32[]{:S(2)}) copy-start(bf16[16,32,128]{2,1,0:T(8,128)(2,1)S(1)} %collective-permute-done.low) | copy-start | bytes 393220
  17.6 0.6 copy-start.1
  64.1 3.5 %collective-permute-start.2 = (bf16[16,32,128]{2,1,0:T(8,128)(2,1)}, bf16[16,32,128]{2,1,0:T(8,128)(2,1)S(1)}, u32[]{:S(2)}, u32[]{:S(2)}) collective-permute-start(bf16[16,32,128]{2,1,0:T(8,128)(2,1)} %get-tuple-element.18), channel_id=1, source_target_pairs={{0,8},{8,16},{16,24},{24,32},{32,40},{40,48},{48,56},{56,64},{64,7... | collective-permute-start | bytes 393224 | tf_op jit(solution)/shard_map/ppermute | solution.py:44
  65.5 5.9 %collective-permute-start.3 = (bf16[16,32,128]{2,1,0:T(8,128)(2,1)}, bf16[16,32,128]{2,1,0:T(8,128)(2,1)S(1)}, u32[]{:S(2)}, u32[]{:S(2)}) collective-permute-start(bf16[16,32,128]{2,1,0:T(8,128)(2,1)} %get-tuple-element.19), channel_id=1, source_target_pairs={{8,0},{16,8},{24,16},{32,24},{40,32},{48,40},{56,48},{64,56},{72,6... | collective-permute-start | bytes 393224 | tf_op jit(solution)/shard_map/ppermute | solution.py:45
  67.7 3.7 %copy-start.3 = (bf16[16,32,128]{2,1,0:T(8,128)(2,1)}, bf16[16,32,128]{2,1,0:T(8,128)(2,1)S(1)}, u32[]{:S(2)}) copy-start(bf16[16,32,128]{2,1,0:T(8,128)(2,1)S(1)} %collective-permute-done.2.low) | copy-start | bytes 393220
  71.4 0.6 copy-start.5
  108.5 3.9 %collective-permute-start.4 = (bf16[16,32,128]{2,1,0:T(8,128)(2,1)}, bf16[16,32,128]{2,1,0:T(8,128)(2,1)S(1)}, u32[]{:S(2)}, u32[]{:S(2)}) collective-permute-start(bf16[16,32,128]{2,1,0:T(8,128)(2,1)} %get-tuple-element.21), channel_id=1, source_target_pairs={{0,8},{8,16},{16,24},{24,32},{32,40},{40,48},{48,56},{56,64},{64,7... | collective-permute-start | bytes 393224 | tf_op jit(solution)/shard_map/ppermute | solution.py:44
  110.2 5.9 %collective-permute-start.5 = (bf16[16,32,128]{2,1,0:T(8,128)(2,1)}, bf16[16,32,128]{2,1,0:T(8,128)(2,1)S(1)}, u32[]{:S(2)}, u32[]{:S(2)}) collective-permute-start(bf16[16,32,128]{2,1,0:T(8,128)(2,1)} %get-tuple-element.23), channel_id=1, source_target_pairs={{8,0},{16,8},{24,16},{32,24},{40,32},{48,40},{56,48},{64,56},{72,6... | collective-permute-start | bytes 393224 | tf_op jit(solution)/shard_map/ppermute | solution.py:45
  112.4 3.7 %copy-start.2 = (bf16[16,32,128]{2,1,0:T(8,128)(2,1)}, bf16[16,32,128]{2,1,0:T(8,128)(2,1)S(1)}, u32[]{:S(2)}) copy-start(bf16[16,32,128]{2,1,0:T(8,128)(2,1)S(1)} %collective-permute-done.4.low) | copy-start | bytes 393220
  116.1 0.6 copy-start.4

commit v2 on v1

v2 whole, which is shorter than its diff:
```python
import jax
import jax.numpy as jnp
import numpy as np
from jax import lax
from jax.experimental import pallas as pl
from jax.experimental.pallas import tpu as pltpu
from jax.sharding import Mesh, PartitionSpec as P

BLK = 128
NBD = 32
HALO = 16
GROUPS = 8
PER_GROUP = NBD // GROUPS
FEATS = 32
BATCH = 8
SIDE_KEY = 16384.0
BF16 = jnp.bfloat16
F32 = jnp.float32

FINE = {"x": 4, "zhi": 8, "zlo": 4, "y": 4, "core": 2}
NODE = ("x", "zhi", "zlo")
FEAT = ("y", "core")
PLANE = ("x", "y", "core")

SMEM = pl.BlockSpec(memory_space=pltpu.SMEM)
VMEM = pl.BlockSpec(memory_space=pltpu.VMEM)
PARAMS = pltpu.CompilerParams(vmem_limit_bytes=16 * 2**20)


def blocks_of(dtype=BF16):
    return jax.ShapeDtypeStruct((NBD, FEATS, BLK), dtype)


def halo_blocks():
    return jax.ShapeDtypeStruct((HALO, FEATS, BLK), BF16)


def exchange(array, axes):
    return lax.all_to_all(array, axes, split_axis=0, concat_axis=0, tiled=True)


def halo(send_low, send_high):
    count = lax.axis_size(NODE)
    forward = [(i, i + 1) for i in range(count - 1)]
    backward = [(target, source) for source, target in forward]
    low = lax.ppermute(send_high, NODE, forward)
    high = lax.ppermute(send_low, NODE, backward)
    return low, high


def turned(row):
    return jnp.transpose(jnp.broadcast_to(row, (BLK, row.shape[1])))


def rank(key, side):
    before = turned(key)
    earlier = (before < key) & (before >= side * SIDE_KEY)
    return jnp.sum(jnp.where(earlier, 1.0, 0.0), axis=0, keepdims=True)


def slot_tables(rows, cols, count, base):
    slot = lax.broadcasted_iota(jnp.int32, rows.shape, 1)
    live = slot < count
    local = (cols - base).astype(F32)
    rows = rows.astype(F32)
    low = live & (local < 0.0)
    high = live & (local >= float(NBD))
    side = jnp.where(low, 1.0, jnp.where(high, 2.0, 0.0))
    offset = side * SIDE_KEY
    shifted = local + float(NBD)
    send_rank = rank(offset + rows * BLK + shifted, side)
    recv_rank = rank(offset + shifted * BLK + rows, side)
    place = jnp.where(side > 0.0, (side - 1.0) * HALO + send_rank, float(BLK))
    lane = lax.broadcasted_iota(jnp.int32, (BLK, BLK), 1).astype(F32)
    send = jnp.sum(jnp.where(turned(place) == lane, turned(rows), 0.0), axis=0, keepdims=True)
    own = jnp.where(live, HALO + local, float(HALO))
    source = jnp.where(low, recv_rank, jnp.where(high, HALO + NBD + recv_rank, own))
    target = jnp.where(live, rows, float(NBD))
    return send.astype(jnp.int32), source.astype(jnp.int32), target.astype(jnp.int32)


def sigmoid(values):
    return 1.0 / (1.0 + jnp.exp(-values))


def gather_sends(tables, blocks, low, high):
    for k in range(HALO):
        low[k] = blocks[tables[0, k]]
        high[k] = blocks[tables[0, HALO + k]]


def split_kernel(scalars, rows, cols, source, tables, blocks, low, high, scalar_tables, done):
    found = slot_tables(rows[...], cols[...], scalars[0], scalars[1])
    tables[...] = jnp.zeros_like(tables)
    for place, table in enumerate(found):
        tables[place : place + 1] = table
    copy = pltpu.make_async_copy(tables, scalar_tables, done)
    copy.start()
    for b in range(NBD):
        blocks[b] = source[:, b * BLK : (b + 1) * BLK]
    copy.wait()
    gather_sends(scalar_tables, blocks, low, high)


def split_blocks(scalars, rows, cols, source):
    return pl.pallas_call(
        split_kernel,
        in_specs=[SMEM, VMEM, VMEM, VMEM],
        out_specs=[VMEM] * 4,
        out_shape=[
            jax.ShapeDtypeStruct((8, BLK), jnp.int32),
            blocks_of(),
            halo_blocks(),
            halo_blocks(),
        ],
        scratch_shapes=[pltpu.SMEM((8, BLK), jnp.int32), pltpu.SemaphoreType.DMA],
        compiler_params=PARAMS,
        name="split_blocks",
    )(scalars, rows, cols, source)


def sends_kernel(tables, blocks, low, high):
    gather_sends(tables, blocks, low, high)


def sends_of(tables, blocks):
    return pl.pallas_call(
        sends_kernel,
        in_specs=[SMEM, VMEM],
        out_specs=[VMEM] * 2,
        out_shape=[halo_blocks(), halo_blocks()],
        compiler_params=PARAMS,
        name="sends_of",
    )(tables, blocks)


def apply_kernel(tables, low, own, high, adj, out, held, total):
    held[0:HALO] = low[...]
    held[HALO : HALO + NBD] = own[...]
    held[HALO + NBD :] = high[...]
    total[...] = jnp.zeros_like(total)
    for start in range(0, adj.shape[0], BATCH):
        slots = range(start, start + BATCH)
        parts = [
            lax.dot_general(
                held[tables[1, m]], adj[m], (((1,), (1,)), ((), ())), preferred_element_type=F32
            )
            for m in slots
        ]
        for m, part in zip(slots, parts):
            row = tables[2, m]
            total[row] = total[row] + part
    out[...] = total[0:NBD].astype(BF16)


def apply_blocks(tables, low, own, high, adj):
    return pl.pallas_call(
        apply_kernel,
        in_specs=[SMEM] + [VMEM] * 4,
        out_specs=VMEM,
        out_shape=blocks_of(),
        scratch_shapes=[
            pltpu.VMEM((2 * HALO + NBD, FEATS, BLK), BF16),
            pltpu.VMEM((NBD + 1, FEATS, BLK), F32),
        ],
        compiler_params=PARAMS,
        name="apply_blocks",
    )(tables, low, own, high, adj)


def rows_of(ref):
    parts = []
    for b in range(PER_GROUP):
        parts.append(
            jnp.concatenate([ref[g * PER_GROUP + b] for g in range(GROUPS)], axis=0)
        )
    return jnp.concatenate(parts, axis=1)


def put_rows(ref, values):
    for g in range(GROUPS):
        for b in range(PER_GROUP):
            ref[g * PER_GROUP + b] = values[
                g * FEATS : (g + 1) * FEATS, b * BLK : (b + 1) * BLK
            ]


def mix_one_kernel(spread, weight, hidden, slope):
    pre = lax.dot_general(
        weight[...], rows_of(spread), (((0,), (0,)), ((), ())), preferred_element_type=F32
    )
    sigma = sigmoid(pre)
    put_rows(hidden, (pre * sigma).astype(BF16))
    slope[...] = sigma * (1.0 + pre * (1.0 - sigma))


def mix_one(spread, weight):
    shape = (GROUPS * FEATS, PER_GROUP * BLK)
    return pl.pallas_call(
        mix_one_kernel,
        in_specs=[VMEM] * 2,
        out_specs=[VMEM] * 2,
        out_shape=[blocks_of(), jax.ShapeDtypeStruct(shape, F32)],
        compiler_params=PARAMS,
        name="mix_one",
    )(spread, weight)


def mix_two_kernel(spread, weight, pre_two):
    pre = lax.dot_general(
        weight[...], rows_of(spread), (((0,), (0,)), ((), ())), preferred_element_type=F32
    )
    put_rows(pre_two, pre.astype(BF16))


def mix_two(spread, weight):
    return pl.pallas_call(
        mix_two_kernel,
        in_specs=[VMEM] * 2,
        out_specs=VMEM,
        out_shape=blocks_of(),
        compiler_params=PARAMS,
        name="mix_two",
    )(spread, weight)


def turn_kernel(tables, pre_two, cotangent, hidden_out, delta, low, high):
    for b in range(NBD):
        span = slice(b * BLK, (b + 1) * BLK)
        pre = pre_two[b].astype(F32)
        sigma = sigmoid(pre)
        hidden_out[:, span] = (pre * sigma).astype(BF16)
        slope = sigma * (1.0 + pre * (1.0 - sigma))
        delta[b] = (cotangent[:, span].astype(F32) * slope).astype(BF16)
    gather_sends(tables, delta, low, high)


def turn(tables, pre_two, cotangent):
    return pl.pallas_call(
        turn_kernel,
        in_specs=[SMEM, VMEM, VMEM],
        out_specs=[VMEM] * 4,
        out_shape=[
            jax.ShapeDtypeStruct(cotangent.shape, BF16),
            blocks_of(),
            halo_blocks(),
            halo_blocks(),
        ],
        compiler_params=PARAMS,
        name="turn",
    )(tables, pre_two, cotangent)


def piece_places():
    for grad in range(2):
        for half in range(2):
            for part in range(GROUPS):
                place = (2 * grad + half) * GROUPS + part
                yield place, grad, slice(part * FEATS, (part + 1) * FEATS), slice(
                    half * BLK, (half + 1) * BLK
                )


def grads_kernel(back_two, spread_one, hidden_one, slope, weight, out):
    back = rows_of(back_two)
    along = (((1,), (1,)), ((), ()))
    carry = jnp.dot(weight[...], back, preferred_element_type=F32).astype(BF16)
    delta = (carry.astype(F32) * slope[...]).astype(BF16)
    sums = (
        lax.dot_general(rows_of(spread_one), delta, along, preferred_element_type=F32),
        lax.dot_general(rows_of(hidden_one), back, along, preferred_element_type=F32),
    )
    for place, grad, rows, columns in piece_places():
        out[place] = sums[grad][rows, columns].astype(BF16)


def grads(back_two, spread_one, hidden_one, slope, weight):
    return pl.pallas_call(
        grads_kernel,
        in_specs=[VMEM] * 5,
        out_specs=VMEM,
        out_shape=blocks_of(),
        compiler_params=PARAMS,
        name="grads",
    )(back_two, spread_one, hidden_one, slope, weight)


def finish_kernel(pieces, grad_one, grad_two):
    outs = (grad_one, grad_two)
    for place, grad, rows, columns in piece_places():
        outs[grad][rows, columns] = pieces[place].astype(F32)


def finish(pieces):
    size = GROUPS * FEATS
    return pl.pallas_call(
        finish_kernel,
        in_specs=[VMEM],
        out_specs=[VMEM] * 2,
        out_shape=[jax.ShapeDtypeStruct((size, size), F32)] * 2,
        compiler_params=PARAMS,
        name="finish",
    )(pieces)


def gather_pieces(piece, axes):
    spread = jnp.broadcast_to(piece[None], (lax.axis_size(axes),) + piece.shape)
    return exchange(spread, axes)


def sum_everywhere(partial):
    pieces = exchange(partial, PLANE).reshape(lax.axis_size(PLANE), -1, BLK)
    piece = jnp.sum(pieces.astype(F32), axis=0)
    piece = jnp.sum(gather_pieces(piece, "zlo"), axis=0).astype(BF16)
    piece = jnp.sum(gather_pieces(piece, "zhi").astype(F32), axis=0).astype(BF16)
    return gather_pieces(piece, PLANE).reshape(partial.shape)


def shards(
    features,
    weight_one,
    weight_two,
    blk_rows,
    blk_cols,
    blk_counts,
    adj_values,
    adj_tvalues,
    cotangent,
):
    base = lax.axis_index(NODE).astype(jnp.int32) * NBD
    scalars = jnp.stack([blk_counts[0], base])
    tables, own, low, high = split_blocks(scalars, blk_rows, blk_cols, features)
    low, high = halo(low, high)
    spread_one = exchange(apply_blocks(tables, low, own, high, adj_values), FEAT)
    hidden_rows, slope_one = mix_one(spread_one, weight_one)
    own = exchange(hidden_rows, FEAT)
    low, high = halo(*sends_of(tables, own))
    spread_two = exchange(apply_blocks(tables, low, own, high, adj_values), FEAT)
    pre_two = exchange(mix_two(spread_two, weight_two), FEAT)
    hidden_out, delta_two, low, high = turn(tables, pre_two, cotangent)
    low, high = halo(low, high)
    back_two = exchange(apply_blocks(tables, low, delta_two, high, adj_tvalues), FEAT)
    partial = grads(back_two, spread_one, hidden_rows, slope_one, weight_two)
    grad_one, grad_two = finish(sum_everywhere(partial))
    return (hidden_out, grad_one, grad_two)


def solution(mesh):
    fine = Mesh(np.asarray(mesh.devices).reshape(tuple(FINE.values())), tuple(FINE))
    return jax.shard_map(
        shards,
        mesh=fine,
        in_specs=(
            P(FEAT, NODE),
            P(),
            P(),
            P(NODE, None),
            P(NODE, None),
            P(NODE),
            P(NODE, None, None),
            P(NODE, None, None),
            P(FEAT, NODE),
        ),
        out_specs=(P(FEAT, NODE), P(), P()),
        check_vma=False,
    )
```

time: 226 us -> 192 us (0.85)
  Pallas kernels: 36 us -> 14.7 us
  blocking collectives: 153 us -> 146 us
  other arithmetic: 4.65 us -> 0.15 us
    pallas_call x4 -> x5, Pallas kernels: 25.4 us -> 11.3 us  [the longest x3 9.13 us: apply_blocks(): pl.pallas_call(apply_kernel, in_specs=[SMEM] + [VMEM] * 4, out_specs=VMEM...]
    all_to_all x9, blocking collectives: 153 us -> 146 us  [exchange(): return lax.all_to_all(array, axes, split_axis=0, concat_axis=0, tiled=True)]
    unnamed x12 -> x18, local copies, waits for them, and re-layouts: 1.93 us -> 4.47 us
where the time goes in v2:
time: 192 us
  blocking collectives  146 us (76%)
  Pallas kernels  14.7 us (8%)
  waiting for transfers between devices  13.4 us (7%)
  starting transfers between devices  11.2 us (6%)
  local copies, waits for them, and re-layouts  4.53 us (2%)
    all_to_all x9, blocking collectives, exchange(): return lax.all_to_all(array, axes, split_axis=0, concat_axis=0, tiled=True)  146 us
    ppermute x3, waiting for transfers between devices, halo(): high = lax.ppermute(send_low, NODE, backward)  11.5 us
    pallas_call x3, Pallas kernels, apply_blocks(): pl.pallas_call(apply_kernel, in_specs=[SMEM] + [VMEM] * 4, out_specs=VMEM...  9.13 us
    ppermute x3, starting transfers between devices, halo(): low = lax.ppermute(send_high, NODE, forward)  7.3 us
    unnamed x18, local copies, waits for them, and re-layouts  4.47 us
    ppermute x3, starting transfers between devices, halo(): high = lax.ppermute(send_low, NODE, backward)  3.88 us
  transfers between devices with their start and end apart: 6, of which 6 were waited for; matrix products, arithmetic and copies ran while one was open for 0% of the time, Pallas kernels for 0%

profile of v2, /device:TPU:1, one launch (start us, length us, event | category | flops | bytes accessed | tf_op | source)
XLA Modules:
  0.0 191.8 jit_solution(6593056992597819152)
XLA Ops:
  1.4 0.9 copy-done.4
  2.3 0.7 copy-done.7
  3.0 0.7 copy-done.8
  3.6 1.4 split_blocks.1
  5.0 4.4 %collective-permute-start = (bf16[16,32,128]{2,1,0:T(8,128)(2,1)S(1)}, bf16[16,32,128]{2,1,0:T(8,128)(2,1)S(1)}, u32[]{:S(2)}, u32[]{:S(2)}) collective-permute-start(bf16[16,32,128]{2,1,0:T(8,128)(2,1)S(1)} %get-tuple-element.18), channel_id=1, source_target_pairs={{0,8},{8,16},{16,24},{24,32},{32,40},{40,48},{48,56},{56,64},{64,7... | collective-permute-start | bytes 393224 | tf_op jit(solution)/shard_map/ppermute | solution.py:46
  9.4 1.3 collective-permute-start.1
  10.7 0.6 collective-permute-done.low
  11.3 4.0 %collective-permute-done.1.high = bf16[16,32,128]{2,1,0:T(8,128)(2,1)S(1)} collective-permute-done((bf16[16,32,128]{2,1,0:T(8,128)(2,1)S(1)}, bf16[16,32,128]{2,1,0:T(8,128)(2,1)S(1)}, u32[]{:S(2)}, u32[]{:S(2)}) %collective-permute-start.1) | collective-permute-done | bytes 131104 | tf_op jit(solution)/shard_map/ppermute | solution.py:47
  15.3 2.2 %copy-done = bf16[128,128,128]{2,1,0:T(8,128)(2,1)S(1)} copy-done((bf16[128,128,128]{2,1,0:T(8,128)(2,1)S(1)}, bf16[128,128,128]{2,1,0:T(8,128)(2,1)}, u32[]{:S(2)}) %copy-start) | copy-done | bytes 4194328
  17.5 3.0 %apply_blocks.3 = bf16[32,32,128]{2,1,0:T(8,128)(2,1)S(1)} custom-call(s32[8,128]{1,0:T(8,128)S(1)} %get-tuple-element.17.tables, bf16[16,32,128]{2,1,0:T(8,128)(2,1)S(1)} %collective-permute-done.low, bf16[32,32,128]{2,1,0:T(8,128)(2,1)S(1)} %get-tuple-element.19.own, bf16[16,32,128]{2,1,0:T(8,128)(2,1)S(1)} %collective-permute-done.1.high, ...), custom_call_target="tpu_custom_call" | custom-call | tf_op jit(solution)/shard_map/apply_blocks/pallas_call | solution.py:157
  20.6 21.1 %all_to_all.45.spread.spread_one = bf16[32,32,128]{2,1,0:T(8,128)(2,1)S(1)} all-to-all(bf16[32,32,128]{2,1,0:T(8,128)(2,1)S(1)} %apply_blocks.3), channel_id=1, replica_groups=mesh['x'=4,'zhi'=8,'zlo'=4,'y'=4,'core'=2] {'y','core'}, dimensions={0} | all-to-all | bytes 524288 | tf_op jit(solution)/shard_map/all_to_all | solution.py:39
  42.1 10.2 %all_to_all.46.blocks.own = bf16[32,32,128]{2,1,0:T(8,128)(2,1)S(1)} all-to-all(bf16[32,32,128]{2,1,0:T(8,128)(2,1)S(1)} %get-tuple-element.21.hidden_one), channel_id=1, replica_groups=mesh['x'=4,'zhi'=8,'zlo'=4,'y'=4,'core'=2] {'y','core'}, dimensions={0} | all-to-all | bytes 524288 | tf_op jit(solution)/shard_map/all_to_all | solution.py:39
  52.3 0.6 sends_of.1
  52.9 1.3 collective-permute-start.2
  54.2 1.3 collective-permute-start.3
  55.5 0.6 collective-permute-done.2.low
  56.1 3.8 %collective-permute-done.3.high = bf16[16,32,128]{2,1,0:T(8,128)(2,1)S(1)} collective-permute-done((bf16[16,32,128]{2,1,0:T(8,128)(2,1)S(1)}, bf16[16,32,128]{2,1,0:T(8,128)(2,1)S(1)}, u32[]{:S(2)}, u32[]{:S(2)}) %collective-permute-start.3) | collective-permute-done | bytes 131104 | tf_op jit(solution)/shard_map/ppermute | solution.py:47
  59.9 3.0 %apply_blocks.4 = bf16[32,32,128]{2,1,0:T(8,128)(2,1)S(1)} custom-call(s32[8,128]{1,0:T(8,128)S(1)} %get-tuple-element.17.tables, bf16[16,32,128]{2,1,0:T(8,128)(2,1)S(1)} %collective-permute-done.2.low, bf16[32,32,128]{2,1,0:T(8,128)(2,1)S(1)} %all_to_all.46.blocks.own, bf16[16,32,128]{2,1,0:T(8,128)(2,1)S(1)} %collective-permute-done.3.high, ...), custom_call_target="tpu_custom_call" | custom-call | tf_op jit(solution)/shard_map/apply_blocks/pallas_call | solution.py:157
  63.0 11.3 %all_to_all.47.spread = bf16[32,32,128]{2,1,0:T(8,128)(2,1)S(1)} all-to-all(bf16[32,32,128]{2,1,0:T(8,128)(2,1)S(1)} %apply_blocks.4), channel_id=1, replica_groups=mesh['x'=4,'zhi'=8,'zlo'=4,'y'=4,'core'=2] {'y','core'}, dimensions={0} | all-to-all | bytes 524288 | tf_op jit(solution)/shard_map/all_to_all | solution.py:39
  74.5 9.9 %all_to_all.48.pre_two = bf16[32,32,128]{2,1,0:T(8,128)(2,1)S(1)} all-to-all(bf16[32,32,128]{2,1,0:T(8,128)(2,1)S(1)} %mix_two.1), channel_id=1, replica_groups=mesh['x'=4,'zhi'=8,'zlo'=4,'y'=4,'core'=2] {'y','core'}, dimensions={0} | all-to-all | bytes 524288 | tf_op jit(solution)/shard_map/all_to_all | solution.py:39
  84.5 1.6 turn.1
  86.0 1.6 collective-permute-start.4
  87.7 1.3 collective-permute-start.5
  89.0 0.6 collective-permute-done.4.low
  89.6 3.8 %collective-permute-done.5.high = bf16[16,32,128]{2,1,0:T(8,128)(2,1)S(1)} collective-permute-done((bf16[16,32,128]{2,1,0:T(8,128)(2,1)S(1)}, bf16[16,32,128]{2,1,0:T(8,128)(2,1)S(1)}, u32[]{:S(2)}, u32[]{:S(2)}) %collective-permute-start.5) | collective-permute-done | bytes 131104 | tf_op jit(solution)/shard_map/ppermute | solution.py:47
  93.4 3.0 %apply_blocks.5 = bf16[32,32,128]{2,1,0:T(8,128)(2,1)S(1)} custom-call(s32[8,128]{1,0:T(8,128)S(1)} %get-tuple-element.17.tables, bf16[16,32,128]{2,1,0:T(8,128)(2,1)S(1)} %collective-permute-done.4.low, bf16[32,32,128]{2,1,0:T(8,128)(2,1)S(1)} %get-tuple-element.26.own, bf16[16,32,128]{2,1,0:T(8,128)(2,1)S(1)} %collective-permute-done.5.high, ...), custom_call_target="tpu_custom_call" | custom-call | tf_op jit(solution)/shard_map/apply_blocks/pallas_call | solution.py:157
  96.4 11.4 %all_to_all.49.back_two = bf16[32,32,128]{2,1,0:T(8,128)(2,1)S(1)} all-to-all(bf16[32,32,128]{2,1,0:T(8,128)(2,1)S(1)} %apply_blocks.5), channel_id=1, replica_groups=mesh['x'=4,'zhi'=8,'zlo'=4,'y'=4,'core'=2] {'y','core'}, dimensions={0} | all-to-all | bytes 524288 | tf_op jit(solution)/shard_map/all_to_all | solution.py:39
  108.3 23.9 %all_to_all.50 = bf16[32,32,128]{2,1,0:T(8,128)(2,1)S(1)} all-to-all(bf16[32,32,128]{2,1,0:T(8,128)(2,1)S(1)} %grads.1), channel_id=1, replica_groups=mesh['x'=4,'zhi'=8,'zlo'=4,'y'=4,'core'=2] {'x','y','core'}, dimensions={0} | all-to-all | bytes 524288 | tf_op jit(solution)/shard_map/all_to_all | solution.py:39
  132.2 7.1 %all_to_all.51 = f32[4,32,128]{2,1,0:T(8,128)S(1)} all-to-all(f32[4,32,128]{2,1,0:T(8,128)S(1)} %broadcast_in_dim.6), channel_id=1, replica_groups=mesh['x'=4,'zhi'=8,'zlo'=4,'y'=4,'core'=2] {'zlo'}, dimensions={0} | all-to-all | bytes 131072 | tf_op jit(solution)/shard_map/all_to_all | solution.py:39
  139.3 36.9 %all_to_all.52 = bf16[8,32,128]{2,1,0:T(8,128)(2,1)S(1)} all-to-all(bf16[8,32,128]{2,1,0:T(8,128)(2,1)S(1)} %broadcast_in_dim.7), channel_id=1, replica_groups=mesh['x'=4,'zhi'=8,'zlo'=4,'y'=4,'core'=2] {'zhi'}, dimensions={0} | all-to-all | bytes 131072 | tf_op jit(solution)/shard_map/all_to_all | solution.py:39
  176.3 14.7 %all_to_all.53.pieces = bf16[32,32,128]{2,1,0:T(8,128)(2,1)S(1)} all-to-all(bf16[32,32,128]{2,1,0:T(8,128)(2,1)S(1)} %broadcast_in_dim.8), channel_id=1, replica_groups=mesh['x'=4,'zhi'=8,'zlo'=4,'y'=4,'core'=2] {'x','y','core'}, dimensions={0} | all-to-all | bytes 524288 | tf_op jit(solution)/shard_map/all_to_all | solution.py:39
  190.9 0.8 finish.1
  (24 shorter events, 1.4 us)
Async XLA Ops:
  1.4 1.0 copy-start.4
  2.3 0.7 copy-start.7
  3.0 0.7 copy-start.8
  3.6 38.0 %copy-start.6 = (bf16[256,256]{1,0:T(8,128)(2,1)S(1)}, bf16[256,256]{1,0:T(8,128)(2,1)}, u32[]{:S(2)}) copy-start(bf16[256,256]{1,0:T(8,128)(2,1)} %weight.3) | copy-start | bytes 393220
  5.0 6.3 %collective-permute-start = (bf16[16,32,128]{2,1,0:T(8,128)(2,1)S(1)}, bf16[16,32,128]{2,1,0:T(8,128)(2,1)S(1)}, u32[]{:S(2)}, u32[]{:S(2)}) collective-permute-start(bf16[16,32,128]{2,1,0:T(8,128)(2,1)S(1)} %get-tuple-element.18), channel_id=1, source_target_pairs={{0,8},{8,16},{16,24},{24,32},{32,40},{40,48},{48,56},{56,64},{64,7... | collective-permute-start | bytes 393224 | tf_op jit(solution)/shard_map/ppermute | solution.py:46
  9.4 5.9 %collective-permute-start.1 = (bf16[16,32,128]{2,1,0:T(8,128)(2,1)S(1)}, bf16[16,32,128]{2,1,0:T(8,128)(2,1)S(1)}, u32[]{:S(2)}, u32[]{:S(2)}) collective-permute-start(bf16[16,32,128]{2,1,0:T(8,128)(2,1)S(1)} %get-tuple-element.20), channel_id=1, source_target_pairs={{8,0},{16,8},{24,16},{32,24},{40,32},{48,40},{56,48},{64,56},{72,6... | collective-permute-start | bytes 393224 | tf_op jit(solution)/shard_map/ppermute | solution.py:47
  15.3 2.2 %copy-start = (bf16[128,128,128]{2,1,0:T(8,128)(2,1)S(1)}, bf16[128,128,128]{2,1,0:T(8,128)(2,1)}, u32[]{:S(2)}) copy-start(bf16[128,128,128]{2,1,0:T(8,128)(2,1)} %adj.4) | copy-start | bytes 12582916
  17.5 42.4 %copy-start.1 = (bf16[128,128,128]{2,1,0:T(8,128)(2,1)S(1)}, bf16[128,128,128]{2,1,0:T(8,128)(2,1)}, u32[]{:S(2)}) copy-start(bf16[128,128,128]{2,1,0:T(8,128)(2,1)} %adj.4) | copy-start | bytes 12582916
  20.6 53.7 %copy-start.3 = (bf16[256,256]{1,0:T(8,128)(2,1)S(1)}, bf16[256,256]{1,0:T(8,128)(2,1)}, u32[]{:S(2)}) copy-start(bf16[256,256]{1,0:T(8,128)(2,1)} %weight.5) | copy-start | bytes 393220
  20.6 63.9 %copy-start.5 = (bf16[32,4096]{1,0:T(8,128)(2,1)S(1)}, bf16[32,4096]{1,0:T(8,128)(2,1)}, u32[]{:S(2)}) copy-start(bf16[32,4096]{1,0:T(8,128)(2,1)} %cotangent.1) | copy-start | bytes 786436
  41.7 51.7 %copy-start.2 = (bf16[128,128,128]{2,1,0:T(8,128)(2,1)S(1)}, bf16[128,128,128]{2,1,0:T(8,128)(2,1)}, u32[]{:S(2)}) copy-start(bf16[128,128,128]{2,1,0:T(8,128)(2,1)} %adj.5) | copy-start | bytes 12582916
  52.9 3.2 %collective-permute-start.2 = (bf16[16,32,128]{2,1,0:T(8,128)(2,1)S(1)}, bf16[16,32,128]{2,1,0:T(8,128)(2,1)S(1)}, u32[]{:S(2)}, u32[]{:S(2)}) collective-permute-start(bf16[16,32,128]{2,1,0:T(8,128)(2,1)S(1)} %get-tuple-element.22), channel_id=1, source_target_pairs={{0,8},{8,16},{16,24},{24,32},{32,40},{40,48},{48,56},{56,64},{64,7... | collective-permute-start | bytes 393224 | tf_op jit(solution)/shard_map/ppermute | solution.py:46
  54.2 5.7 %collective-permute-start.3 = (bf16[16,32,128]{2,1,0:T(8,128)(2,1)S(1)}, bf16[16,32,128]{2,1,0:T(8,128)(2,1)S(1)}, u32[]{:S(2)}, u32[]{:S(2)}) collective-permute-start(bf16[16,32,128]{2,1,0:T(8,128)(2,1)S(1)} %get-tuple-element.23), channel_id=1, source_target_pairs={{8,0},{16,8},{24,16},{32,24},{40,32},{48,40},{56,48},{64,56},{72,6... | collective-permute-start | bytes 393224 | tf_op jit(solution)/shard_map/ppermute | solution.py:47
  86.0 3.6 %collective-permute-start.4 = (bf16[16,32,128]{2,1,0:T(8,128)(2,1)S(1)}, bf16[16,32,128]{2,1,0:T(8,128)(2,1)S(1)}, u32[]{:S(2)}, u32[]{:S(2)}) collective-permute-start(bf16[16,32,128]{2,1,0:T(8,128)(2,1)S(1)} %get-tuple-element.25), channel_id=1, source_target_pairs={{0,8},{8,16},{16,24},{24,32},{32,40},{40,48},{48,56},{56,64},{64,7... | collective-permute-start | bytes 393224 | tf_op jit(solution)/shard_map/ppermute | solution.py:46
  87.7 5.7 %collective-permute-start.5 = (bf16[16,32,128]{2,1,0:T(8,128)(2,1)S(1)}, bf16[16,32,128]{2,1,0:T(8,128)(2,1)S(1)}, u32[]{:S(2)}, u32[]{:S(2)}) collective-permute-start(bf16[16,32,128]{2,1,0:T(8,128)(2,1)S(1)} %get-tuple-element.27), channel_id=1, source_target_pairs={{8,0},{16,8},{24,16},{32,24},{40,32},{48,40},{56,48},{64,56},{72,6... | collective-permute-start | bytes 393224 | tf_op jit(solution)/shard_map/ppermute | solution.py:47

commit v3 on v2

--- a/solution.py
+++ b/solution.py
@@ -70,13 +70,22 @@
     shifted = local + float(NBD)
     send_rank = rank(offset + rows * BLK + shifted, side)
     recv_rank = rank(offset + shifted * BLK + rows, side)
-    place = jnp.where(side > 0.0, (side - 1.0) * HALO + send_rank, float(BLK))
+    first = jnp.where(side > 0.0, (side - 1.0) * HALO, float(BLK))
     lane = lax.broadcasted_iota(jnp.int32, (BLK, BLK), 1).astype(F32)
-    send = jnp.sum(jnp.where(turned(place) == lane, turned(rows), 0.0), axis=0, keepdims=True)
-    own = jnp.where(live, HALO + local, float(HALO))
-    source = jnp.where(low, recv_rank, jnp.where(high, HALO + NBD + recv_rank, own))
-    target = jnp.where(live, rows, float(NBD))
-    return send.astype(jnp.int32), source.astype(jnp.int32), target.astype(jnp.int32)
+    slots = lax.broadcasted_iota(jnp.int32, (BLK, BLK), 0).astype(F32)
+    rows_down = turned(rows)
+    sent = turned(first + send_rank) == lane
+    received = turned(first + recv_rank) == lane
+    total = lambda hit, values: jnp.sum(jnp.where(hit, values, 0.0), axis=0, keepdims=True)
+    own = live & (side == 0.0)
+    found = (
+        total(sent, rows_down),
+        jnp.where(own, local, 0.0),
+        jnp.where(own, rows, float(NBD)),
+        total(received, slots),
+        NBD + total(received, rows_down - NBD),
+    )
+    return [table.astype(jnp.int32) for table in found]
 
 
 def sigmoid(values):
@@ -89,8 +98,8 @@
         high[k] = blocks[tables[0, HALO + k]]
 
 
-def split_kernel(scalars, rows, cols, source, tables, blocks, low, high, scalar_tables, done):
-    found = slot_tables(rows[...], cols[...], scalars[0], scalars[1])
+def split_kernel(slots, source, tables, blocks, low, high, scalar_tables, done):
+    found = slot_tables(slots[0:1], slots[1:2], slots[2:3], slots[3:4])
     tables[...] = jnp.zeros_like(tables)
     for place, table in enumerate(found):
         tables[place : place + 1] = table
@@ -102,10 +111,10 @@
     gather_sends(scalar_tables, blocks, low, high)
 
 
-def split_blocks(scalars, rows, cols, source):
+def split_blocks(slots, source):
     return pl.pallas_call(
         split_kernel,
-        in_specs=[SMEM, VMEM, VMEM, VMEM],
+        in_specs=[VMEM] * 2,
         out_specs=[VMEM] * 4,
         out_shape=[
             jax.ShapeDtypeStruct((8, BLK), jnp.int32),
@@ -116,7 +125,7 @@
         scratch_shapes=[pltpu.SMEM((8, BLK), jnp.int32), pltpu.SemaphoreType.DMA],
         compiler_params=PARAMS,
         name="split_blocks",
-    )(scalars, rows, cols, source)
+    )(slots, source)
 
 
 def sends_kernel(tables, blocks, low, high):
@@ -134,38 +143,60 @@
     )(tables, blocks)
 
 
-def apply_kernel(tables, low, own, high, adj, out, held, total):
-    held[0:HALO] = low[...]
-    held[HALO : HALO + NBD] = own[...]
-    held[HALO + NBD :] = high[...]
+def add_slots(total, batch):
+    parts = [
+        lax.dot_general(block, adj, (((1,), (1,)), ((), ())), preferred_element_type=F32)
+        for block, adj, _ in batch
+    ]
+    for part, (_, _, row) in zip(parts, batch):
+        total[row] = total[row] + part
+
+
+def apply_own_kernel(tables, own, adj, total):
     total[...] = jnp.zeros_like(total)
     for start in range(0, adj.shape[0], BATCH):
         slots = range(start, start + BATCH)
-        parts = [
-            lax.dot_general(
-                held[tables[1, m]], adj[m], (((1,), (1,)), ((), ())), preferred_element_type=F32
-            )
-            for m in slots
-        ]
-        for m, part in zip(slots, parts):
-            row = tables[2, m]
-            total[row] = total[row] + part
+        add_slots(total, [(own[tables[1, m]], adj[m], tables[2, m]) for m in slots])
+
+
+def apply_own(tables, own, adj):
+    return pl.pallas_call(
+        apply_own_kernel,
+        in_specs=[SMEM] + [VMEM] * 2,
+        out_specs=VMEM,
+        out_shape=jax.ShapeDtypeStruct((NBD + 1, FEATS, BLK), F32),
+        compiler_params=PARAMS,
+        name="apply_own",
+    )(tables, own, adj)
+
+
+def apply_halo_kernel(tables, begun, low, high, adj, out, total):
+    total[...] = begun[...]
+    for side, blocks in enumerate((low, high)):
+        for start in range(0, HALO, BATCH):
+            batch = []
+            for k in range(start, start + BATCH):
+                place = side * HALO + k
+                batch.append((blocks[k], adj[tables[3, place]], tables[4, place]))
+            add_slots(total, batch)
     out[...] = total[0:NBD].astype(BF16)
 
 
-def apply_blocks(tables, low, own, high, adj):
-    return pl.pallas_call(
-        apply_kernel,
+def apply_halo(tables, begun, low, high, adj):
+    return pl.pallas_call(
+        apply_halo_kernel,
         in_specs=[SMEM] + [VMEM] * 4,
         out_specs=VMEM,
         out_shape=blocks_of(),
-        scratch_shapes=[
-            pltpu.VMEM((2 * HALO + NBD, FEATS, BLK), BF16),
-            pltpu.VMEM((NBD + 1, FEATS, BLK), F32),
-        ],
-        compiler_params=PARAMS,
-        name="apply_blocks",
-    )(tables, low, own, high, adj)
+        scratch_shapes=[pltpu.VMEM((NBD + 1, FEATS, BLK), F32)],
+        compiler_params=PARAMS,
+        name="apply_halo",
+    )(tables, begun, low, high, adj)
+
+
+def apply_blocks(tables, own, sends, adj):
+    low, high = halo(*sends)
+    return apply_halo(tables, apply_own(tables, own, adj), low, high, adj)
 
 
 def rows_of(ref):
@@ -224,13 +255,12 @@
     )(spread, weight)
 
 
-def turn_kernel(tables, pre_two, cotangent, hidden_out, delta, low, high):
+def turn_kernel(tables, pre_two, cotangent, delta, low, high):
     for b in range(NBD):
-        span = slice(b * BLK, (b + 1) * BLK)
         pre = pre_two[b].astype(F32)
         sigma = sigmoid(pre)
-        hidden_out[:, span] = (pre * sigma).astype(BF16)
         slope = sigma * (1.0 + pre * (1.0 - sigma))
+        span = slice(b * BLK, (b + 1) * BLK)
         delta[b] = (cotangent[:, span].astype(F32) * slope).astype(BF16)
     gather_sends(tables, delta, low, high)
 
@@ -239,16 +269,28 @@
     return pl.pallas_call(
         turn_kernel,
         in_specs=[SMEM, VMEM, VMEM],
-        out_specs=[VMEM] * 4,
-        out_shape=[
-            jax.ShapeDtypeStruct(cotangent.shape, BF16),
-            blocks_of(),
-            halo_blocks(),
-            halo_blocks(),
-        ],
+        out_specs=[VMEM] * 3,
+        out_shape=[blocks_of(), halo_blocks(), halo_blocks()],
         compiler_params=PARAMS,
         name="turn",
     )(tables, pre_two, cotangent)
+
+
+def hidden_kernel(pre_two, hidden_out):
+    for b in range(NBD):
+        pre = pre_two[b].astype(F32)
+        hidden_out[:, b * BLK : (b + 1) * BLK] = (pre * sigmoid(pre)).astype(BF16)
+
+
+def hidden_of(pre_two):
+    return pl.pallas_call(
+        hidden_kernel,
+        in_specs=[VMEM],
+        out_specs=VMEM,
+        out_shape=jax.ShapeDtypeStruct((FEATS, NBD * BLK), BF16),
+        compiler_params=PARAMS,
+        name="hidden_of",
+    )(pre_two)
 
 
 def piece_places():
@@ -328,18 +370,17 @@
     cotangent,
 ):
     base = lax.axis_index(NODE).astype(jnp.int32) * NBD
-    scalars = jnp.stack([blk_counts[0], base])
-    tables, own, low, high = split_blocks(scalars, blk_rows, blk_cols, features)
-    low, high = halo(low, high)
-    spread_one = exchange(apply_blocks(tables, low, own, high, adj_values), FEAT)
+    spread = lambda scalar: jnp.broadcast_to(scalar, blk_rows.shape)
+    slots = jnp.concatenate([blk_rows, blk_cols, spread(blk_counts[0]), spread(base)])
+    tables, own, *sends = split_blocks(slots, features)
+    spread_one = exchange(apply_blocks(tables, own, sends, adj_values), FEAT)
     hidden_rows, slope_one = mix_one(spread_one, weight_one)
     own = exchange(hidden_rows, FEAT)
-    low, high = halo(*sends_of(tables, own))
-    spread_two = exchange(apply_blocks(tables, low, own, high, adj_values), FEAT)
+    spread_two = exchange(apply_blocks(tables, own, sends_of(tables, own), adj_values), FEAT)
     pre_two = exchange(mix_two(spread_two, weight_two), FEAT)
-    hidden_out, delta_two, low, high = turn(tables, pre_two, cotangent)
-    low, high = halo(low, high)
-    back_two = exchange(apply_blocks(tables, low, delta_two, high, adj_tvalues), FEAT)
+    delta_two, *sends = turn(tables, pre_two, cotangent)
+    back_two = exchange(apply_blocks(tables, delta_two, sends, adj_tvalues), FEAT)
+    hidden_out = hidden_of(pre_two)
     partial = grads(back_two, spread_one, hidden_rows, slope_one, weight_two)
     grad_one, grad_two = finish(sum_everywhere(partial))
     return (hidden_out, grad_one, grad_two)

time: 192 us -> 187 us (0.974)
  blocking collectives: 146 us -> 131 us
  starting transfers between devices: 11.2 us -> 19.9 us
  Pallas kernels: 14.7 us -> 17.8 us
  waiting for transfers between devices: 13.4 us -> 11.2 us
    all_to_all x9 -> x8, blocking collectives: 146 us -> 131 us  [exchange(): return lax.all_to_all(array, axes, split_axis=0, concat_axis=0, tiled=True)]
    ppermute x3, waiting for transfers between devices: 11.5 us -> 2.94 us  [halo(): high = lax.ppermute(send_low, NODE, backward)]
    all_to_all x0 -> x1, waiting for transfers between devices: none -> 8.25 us  [exchange(): return lax.all_to_all(array, axes, split_axis=0, concat_axis=0, tiled=True)]
    all_to_all x0 -> x1, starting transfers between devices: none -> 6.07 us  [exchange(): return lax.all_to_all(array, axes, split_axis=0, concat_axis=0, tiled=True)]
    pallas_call x4 -> x8, Pallas kernels: 10.5 us -> 14.4 us  [the longest x3 8.74 us: apply_own(): pl.pallas_call(apply_own_kernel, in_specs=[SMEM] + [VMEM] * 2, out_specs=...]
    ppermute x3, starting transfers between devices: 7.3 us -> 9.87 us  [halo(): low = lax.ppermute(send_high, NODE, forward)]
    unnamed x18 -> x14, local copies, waits for them, and re-layouts: 4.47 us -> 3.16 us
  transfers between devices with their start and end apart: 6 -> 7, of which waited for: 6 -> 3; matrix products, arithmetic and copies ran while one was open for 0% -> 0% of each run, Pallas kernels for 0% -> 5%
where the time goes in v3:
time: 187 us; the launch traced here: 186 us
  blocking collectives  131 us (70%)
  starting transfers between devices  19.9 us (11%)
  Pallas kernels  17.8 us (10%)
  waiting for transfers between devices  11.2 us (6%)
  local copies, waits for them, and re-layouts  4.06 us (2%)
    all_to_all x8, blocking collectives, exchange(): return lax.all_to_all(array, axes, split_axis=0, concat_axis=0, tiled=True)  131 us
    ppermute x3, starting transfers between devices, halo(): low = lax.ppermute(send_high, NODE, forward)  9.87 us
    pallas_call x3, Pallas kernels, apply_own(): pl.pallas_call(apply_own_kernel, in_specs=[SMEM] + [VMEM] * 2, out_specs=...  8.74 us
    all_to_all x1, waiting for transfers between devices, exchange(): return lax.all_to_all(array, axes, split_axis=0, concat_axis=0, tiled=True)  8.25 us
    all_to_all x1, starting transfers between devices, exchange(): return lax.all_to_all(array, axes, split_axis=0, concat_axis=0, tiled=True)  6.07 us
    ppermute x3, starting transfers between devices, halo(): high = lax.ppermute(send_low, NODE, backward)  4.01 us
    pallas_call x3, Pallas kernels, apply_halo(): pl.pallas_call(apply_halo_kernel, in_specs=[SMEM] + [VMEM] * 4, out_specs...  3.9 us
  transfers between devices with their start and end apart: 7, of which 3 were waited for; matrix products, arithmetic and copies ran while one was open for 0% of the time, Pallas kernels for 5%

profile of v3, /device:TPU:1, one launch (start us, length us, event | category | flops | bytes accessed | tf_op | source)
XLA Modules:
  0.0 185.9 jit_solution(17210105970168589683)
XLA Ops:
  1.4 0.7 add_add_fusion.slots
  2.2 0.9 copy-done.4
  3.1 0.9 split_blocks.1
  4.0 4.4 %collective-permute-start = (bf16[16,32,128]{2,1,0:T(8,128)(2,1)S(1)}, bf16[16,32,128]{2,1,0:T(8,128)(2,1)S(1)}, u32[]{:S(2)}, u32[]{:S(2)}) collective-permute-start(bf16[16,32,128]{2,1,0:T(8,128)(2,1)S(1)} %get-tuple-element.18), channel_id=1, source_target_pairs={{0,8},{8,16},{16,24},{24,32},{32,40},{40,48},{48,56},{56,64},{64,7... | collective-permute-start | bytes 393224 | tf_op jit(solution)/shard_map/ppermute | solution.py:46
  8.4 1.3 collective-permute-start.1
  9.7 2.2 %copy-done = bf16[128,128,128]{2,1,0:T(8,128)(2,1)S(1)} copy-done((bf16[128,128,128]{2,1,0:T(8,128)(2,1)S(1)}, bf16[128,128,128]{2,1,0:T(8,128)(2,1)}, u32[]{:S(2)}) %copy-start) | copy-done | bytes 4194328
  11.9 2.9 %apply_own.3.begun = f32[33,32,128]{2,1,0:T(8,128)S(1)} custom-call(s32[8,128]{1,0:T(8,128)S(1)} %get-tuple-element.16.tables, bf16[32,32,128]{2,1,0:T(8,128)(2,1)S(1)} %get-tuple-element.17.own, bf16[128,128,128]{2,1,0:T(8,128)(2,1)S(1)} %copy-done), custom_call_target="tpu_custom_call" | custom-call | tf_op jit(solution)/shard_map/apply_own/pallas_call | solution.py:163
  14.8 1.3 apply_halo.3
  16.1 20.4 %all_to_all.45.spread.spread_one = bf16[32,32,128]{2,1,0:T(8,128)(2,1)S(1)} all-to-all(bf16[32,32,128]{2,1,0:T(8,128)(2,1)S(1)} %apply_halo.3), channel_id=1, replica_groups=mesh['x'=4,'zhi'=8,'zlo'=4,'y'=4,'core'=2] {'y','core'}, dimensions={0} | all-to-all | bytes 524288 | tf_op jit(solution)/shard_map/all_to_all | solution.py:39
  36.9 9.9 %all_to_all.46.own.blocks = bf16[32,32,128]{2,1,0:T(8,128)(2,1)S(1)} all-to-all(bf16[32,32,128]{2,1,0:T(8,128)(2,1)S(1)} %get-tuple-element.20.hidden_one), channel_id=1, replica_groups=mesh['x'=4,'zhi'=8,'zlo'=4,'y'=4,'core'=2] {'y','core'}, dimensions={0} | all-to-all | bytes 524288 | tf_op jit(solution)/shard_map/all_to_all | solution.py:39
  47.5 3.8 %collective-permute-start.2 = (bf16[16,32,128]{2,1,0:T(8,128)(2,1)S(1)}, bf16[16,32,128]{2,1,0:T(8,128)(2,1)S(1)}, u32[]{:S(2)}, u32[]{:S(2)}) collective-permute-start(bf16[16,32,128]{2,1,0:T(8,128)(2,1)S(1)} %get-tuple-element.21), channel_id=1, source_target_pairs={{0,8},{8,16},{16,24},{24,32},{32,40},{40,48},{48,56},{56,64},{64,7... | collective-permute-start | bytes 393224 | tf_op jit(solution)/shard_map/ppermute | solution.py:46
  51.4 1.4 collective-permute-start.3
  52.8 2.9 %apply_own.4.begun = f32[33,32,128]{2,1,0:T(8,128)S(1)} custom-call(s32[8,128]{1,0:T(8,128)S(1)} %get-tuple-element.16.tables, bf16[32,32,128]{2,1,0:T(8,128)(2,1)S(1)} %all_to_all.46.own.blocks, bf16[128,128,128]{2,1,0:T(8,128)(2,1)S(1)} %copy-done.1), custom_call_target="tpu_custom_call" | custom-call | tf_op jit(solution)/shard_map/apply_own/pallas_call | solution.py:163
  55.8 1.5 collective-permute-done.3.high
  57.2 1.3 apply_halo.4
  58.5 11.4 %all_to_all.47.spread = bf16[32,32,128]{2,1,0:T(8,128)(2,1)S(1)} all-to-all(bf16[32,32,128]{2,1,0:T(8,128)(2,1)S(1)} %apply_halo.4), channel_id=1, replica_groups=mesh['x'=4,'zhi'=8,'zlo'=4,'y'=4,'core'=2] {'y','core'}, dimensions={0} | all-to-all | bytes 524288 | tf_op jit(solution)/shard_map/all_to_all | solution.py:39
  70.2 9.9 %all_to_all.48.pre_two = bf16[32,32,128]{2,1,0:T(8,128)(2,1)S(1)} all-to-all(bf16[32,32,128]{2,1,0:T(8,128)(2,1)S(1)} %mix_two.1), channel_id=1, replica_groups=mesh['x'=4,'zhi'=8,'zlo'=4,'y'=4,'core'=2] {'y','core'}, dimensions={0} | all-to-all | bytes 524288 | tf_op jit(solution)/shard_map/all_to_all | solution.py:39
  80.1 0.8 turn.1
  81.0 1.7 collective-permute-start.4
  82.6 1.3 collective-permute-start.5
  83.9 2.9 %apply_own.5.begun = f32[33,32,128]{2,1,0:T(8,128)S(1)} custom-call(s32[8,128]{1,0:T(8,128)S(1)} %get-tuple-element.16.tables, bf16[32,32,128]{2,1,0:T(8,128)(2,1)S(1)} %get-tuple-element.23.own, bf16[128,128,128]{2,1,0:T(8,128)(2,1)S(1)} %copy-done.2), custom_call_target="tpu_custom_call" | custom-call | tf_op jit(solution)/shard_map/apply_own/pallas_call | solution.py:163
  86.9 1.5 collective-permute-done.5.high
  88.3 1.3 apply_halo.5
  89.6 11.4 %all_to_all.49.back_two = bf16[32,32,128]{2,1,0:T(8,128)(2,1)S(1)} all-to-all(bf16[32,32,128]{2,1,0:T(8,128)(2,1)S(1)} %apply_halo.5), channel_id=1, replica_groups=mesh['x'=4,'zhi'=8,'zlo'=4,'y'=4,'core'=2] {'y','core'}, dimensions={0} | all-to-all | bytes 524288 | tf_op jit(solution)/shard_map/all_to_all | solution.py:39
  101.5 23.7 %all_to_all.50 = bf16[32,32,128]{2,1,0:T(8,128)(2,1)S(1)} all-to-all(bf16[32,32,128]{2,1,0:T(8,128)(2,1)S(1)} %grads.1), channel_id=1, replica_groups=mesh['x'=4,'zhi'=8,'zlo'=4,'y'=4,'core'=2] {'x','y','core'}, dimensions={0} | all-to-all | bytes 524288 | tf_op jit(solution)/shard_map/all_to_all | solution.py:39
  125.3 7.1 %all_to_all.51 = f32[4,32,128]{2,1,0:T(8,128)S(1)} all-to-all(f32[4,32,128]{2,1,0:T(8,128)S(1)} %broadcast_in_dim.12), channel_id=1, replica_groups=mesh['x'=4,'zhi'=8,'zlo'=4,'y'=4,'core'=2] {'zlo'}, dimensions={0} | all-to-all | bytes 131072 | tf_op jit(solution)/shard_map/all_to_all | solution.py:39
  132.4 36.7 %all_to_all.52 = bf16[8,32,128]{2,1,0:T(8,128)(2,1)S(1)} all-to-all(bf16[8,32,128]{2,1,0:T(8,128)(2,1)S(1)} %broadcast_in_dim.13), channel_id=1, replica_groups=mesh['x'=4,'zhi'=8,'zlo'=4,'y'=4,'core'=2] {'zhi'}, dimensions={0} | all-to-all | bytes 131072 | tf_op jit(solution)/shard_map/all_to_all | solution.py:39
  169.2 0.7 broadcast_in_dim.28
  169.9 6.1 %all-to-all-start.8 = ((bf16[32,32,128]{2,1,0:T(8,128)(2,1)}), bf16[32,32,128]{2,1,0:T(8,128)(2,1)S(1)}, u32[]{:S(2)}, u32[]{:S(2)}) async-start(bf16[32,32,128]{2,1,0:T(8,128)(2,1)} %broadcast_in_dim.28), calls=%async_computation.8 | async-start | bytes 524288 | tf_op jit(solution)/shard_map/all_to_all | solution.py:39
  176.0 0.9 hidden_of.1
  176.8 8.2 %all-to-all-done.8.pieces = bf16[32,32,128]{2,1,0:T(8,128)(2,1)S(1)} async-done(((bf16[32,32,128]{2,1,0:T(8,128)(2,1)}), bf16[32,32,128]{2,1,0:T(8,128)(2,1)S(1)}, u32[]{:S(2)}, u32[]{:S(2)}) %all-to-all-start.8) | async-done | bytes 262176 | tf_op jit(solution)/shard_map/all_to_all | solution.py:39
  185.1 0.8 finish.1
  (27 shorter events, 2.1 us)
Async XLA Ops:
  2.2 0.9 copy-start.4
  4.0 10.8 %collective-permute-start = (bf16[16,32,128]{2,1,0:T(8,128)(2,1)S(1)}, bf16[16,32,128]{2,1,0:T(8,128)(2,1)S(1)}, u32[]{:S(2)}, u32[]{:S(2)}) collective-permute-start(bf16[16,32,128]{2,1,0:T(8,128)(2,1)S(1)} %get-tuple-element.18), channel_id=1, source_target_pairs={{0,8},{8,16},{16,24},{24,32},{32,40},{40,48},{48,56},{56,64},{64,7... | collective-permute-start | bytes 393224 | tf_op jit(solution)/shard_map/ppermute | solution.py:46
  8.4 6.4 %collective-permute-start.1 = (bf16[16,32,128]{2,1,0:T(8,128)(2,1)S(1)}, bf16[16,32,128]{2,1,0:T(8,128)(2,1)S(1)}, u32[]{:S(2)}, u32[]{:S(2)}) collective-permute-start(bf16[16,32,128]{2,1,0:T(8,128)(2,1)S(1)} %get-tuple-element.19), channel_id=1, source_target_pairs={{8,0},{16,8},{24,16},{32,24},{40,32},{48,40},{56,48},{64,56},{72,6... | collective-permute-start | bytes 393224 | tf_op jit(solution)/shard_map/ppermute | solution.py:47
  9.7 2.2 %copy-start = (bf16[128,128,128]{2,1,0:T(8,128)(2,1)S(1)}, bf16[128,128,128]{2,1,0:T(8,128)(2,1)}, u32[]{:S(2)}) copy-start(bf16[128,128,128]{2,1,0:T(8,128)(2,1)} %adj.9) | copy-start | bytes 12582916
  11.9 2.9 %copy-start.1 = (bf16[128,128,128]{2,1,0:T(8,128)(2,1)S(1)}, bf16[128,128,128]{2,1,0:T(8,128)(2,1)}, u32[]{:S(2)}) copy-start(bf16[128,128,128]{2,1,0:T(8,128)(2,1)} %adj.9) | copy-start | bytes 12582916
  11.9 24.7 %copy-start.6 = (bf16[256,256]{1,0:T(8,128)(2,1)S(1)}, bf16[256,256]{1,0:T(8,128)(2,1)}, u32[]{:S(2)}) copy-start(bf16[256,256]{1,0:T(8,128)(2,1)} %weight.3) | copy-start | bytes 393220
  47.5 8.2 %collective-permute-start.2 = (bf16[16,32,128]{2,1,0:T(8,128)(2,1)S(1)}, bf16[16,32,128]{2,1,0:T(8,128)(2,1)S(1)}, u32[]{:S(2)}, u32[]{:S(2)}) collective-permute-start(bf16[16,32,128]{2,1,0:T(8,128)(2,1)S(1)} %get-tuple-element.21), channel_id=1, source_target_pairs={{0,8},{8,16},{16,24},{24,32},{32,40},{40,48},{48,56},{56,64},{64,7... | collective-permute-start | bytes 393224 | tf_op jit(solution)/shard_map/ppermute | solution.py:46
  51.4 18.5 %copy-start.3 = (bf16[256,256]{1,0:T(8,128)(2,1)S(1)}, bf16[256,256]{1,0:T(8,128)(2,1)}, u32[]{:S(2)}) copy-start(bf16[256,256]{1,0:T(8,128)(2,1)} %weight.5) | copy-start | bytes 393220
  51.4 5.8 %collective-permute-start.3 = (bf16[16,32,128]{2,1,0:T(8,128)(2,1)S(1)}, bf16[16,32,128]{2,1,0:T(8,128)(2,1)S(1)}, u32[]{:S(2)}, u32[]{:S(2)}) collective-permute-start(bf16[16,32,128]{2,1,0:T(8,128)(2,1)S(1)} %get-tuple-element.22), channel_id=1, source_target_pairs={{8,0},{16,8},{24,16},{32,24},{40,32},{48,40},{56,48},{64,56},{72,6... | collective-permute-start | bytes 393224 | tf_op jit(solution)/shard_map/ppermute | solution.py:47
  55.7 24.4 %copy-start.5 = (bf16[32,4096]{1,0:T(8,128)(2,1)S(1)}, bf16[32,4096]{1,0:T(8,128)(2,1)}, u32[]{:S(2)}) copy-start(bf16[32,4096]{1,0:T(8,128)(2,1)} %cotangent.1) | copy-start | bytes 786436
  55.7 28.2 %copy-start.2 = (bf16[128,128,128]{2,1,0:T(8,128)(2,1)S(1)}, bf16[128,128,128]{2,1,0:T(8,128)(2,1)}, u32[]{:S(2)}) copy-start(bf16[128,128,128]{2,1,0:T(8,128)(2,1)} %adj.11) | copy-start | bytes 12582916
  81.0 5.9 %collective-permute-start.4 = (bf16[16,32,128]{2,1,0:T(8,128)(2,1)S(1)}, bf16[16,32,128]{2,1,0:T(8,128)(2,1)S(1)}, u32[]{:S(2)}, u32[]{:S(2)}) collective-permute-start(bf16[16,32,128]{2,1,0:T(8,128)(2,1)S(1)} %get-tuple-element.24), channel_id=1, source_target_pairs={{0,8},{8,16},{16,24},{24,32},{32,40},{40,48},{48,56},{56,64},{64,7... | collective-permute-start | bytes 393224 | tf_op jit(solution)/shard_map/ppermute | solution.py:46
  82.6 5.7 %collective-permute-start.5 = (bf16[16,32,128]{2,1,0:T(8,128)(2,1)S(1)}, bf16[16,32,128]{2,1,0:T(8,128)(2,1)S(1)}, u32[]{:S(2)}, u32[]{:S(2)}) collective-permute-start(bf16[16,32,128]{2,1,0:T(8,128)(2,1)S(1)} %get-tuple-element.25), channel_id=1, source_target_pairs={{8,0},{16,8},{24,16},{32,24},{40,32},{48,40},{56,48},{64,56},{72,6... | collective-permute-start | bytes 393224 | tf_op jit(solution)/shard_map/ppermute | solution.py:47
  169.9 15.2 %all-to-all-start.8 = ((bf16[32,32,128]{2,1,0:T(8,128)(2,1)}), bf16[32,32,128]{2,1,0:T(8,128)(2,1)S(1)}, u32[]{:S(2)}, u32[]{:S(2)}) async-start(bf16[32,32,128]{2,1,0:T(8,128)(2,1)} %broadcast_in_dim.28), calls=%async_computation.8 | async-start | bytes 524288 | tf_op jit(solution)/shard_map/all_to_all | solution.py:39

commit v4 on v3

--- a/solution.py
+++ b/solution.py
@@ -276,21 +276,25 @@
     )(tables, pre_two, cotangent)
 
 
-def hidden_kernel(pre_two, hidden_out):
+def apply_own_hidden_kernel(tables, own, adj, pre_two, total, hidden_out):
+    apply_own_kernel(tables, own, adj, total)
     for b in range(NBD):
         pre = pre_two[b].astype(F32)
         hidden_out[:, b * BLK : (b + 1) * BLK] = (pre * sigmoid(pre)).astype(BF16)
 
 
-def hidden_of(pre_two):
-    return pl.pallas_call(
-        hidden_kernel,
-        in_specs=[VMEM],
-        out_specs=VMEM,
-        out_shape=jax.ShapeDtypeStruct((FEATS, NBD * BLK), BF16),
-        compiler_params=PARAMS,
-        name="hidden_of",
-    )(pre_two)
+def apply_own_hidden(tables, own, adj, pre_two):
+    return pl.pallas_call(
+        apply_own_hidden_kernel,
+        in_specs=[SMEM] + [VMEM] * 3,
+        out_specs=[VMEM] * 2,
+        out_shape=[
+            jax.ShapeDtypeStruct((NBD + 1, FEATS, BLK), F32),
+            jax.ShapeDtypeStruct((FEATS, NBD * BLK), BF16),
+        ],
+        compiler_params=PARAMS,
+        name="apply_own_hidden",
+    )(tables, own, adj, pre_two)
 
 
 def piece_places():
@@ -379,8 +383,9 @@
     spread_two = exchange(apply_blocks(tables, own, sends_of(tables, own), adj_values), FEAT)
     pre_two = exchange(mix_two(spread_two, weight_two), FEAT)
     delta_two, *sends = turn(tables, pre_two, cotangent)
-    back_two = exchange(apply_blocks(tables, delta_two, sends, adj_tvalues), FEAT)
-    hidden_out = hidden_of(pre_two)
+    low, high = halo(*sends)
+    begun, hidden_out = apply_own_hidden(tables, delta_two, adj_tvalues, pre_two)
+    back_two = exchange(apply_halo(tables, begun, low, high, adj_tvalues), FEAT)
     partial = grads(back_two, spread_one, hidden_rows, slope_one, weight_two)
     grad_one, grad_two = finish(sum_everywhere(partial))
     return (hidden_out, grad_one, grad_two)

time: 187 us -> 185 us (0.989)
  blocking collectives: 131 us -> 145 us
  waiting for transfers between devices: 11.2 us -> 2.17 us
  starting transfers between devices: 19.9 us -> 13.9 us
    all_to_all x8 -> x9, blocking collectives: 131 us -> 145 us  [exchange(): return lax.all_to_all(array, axes, split_axis=0, concat_axis=0, tiled=True)]
    all_to_all x1 -> x0, waiting for transfers between devices: 8.25 us -> none  [exchange(): return lax.all_to_all(array, axes, split_axis=0, concat_axis=0, tiled=True)]
    all_to_all x1 -> x0, starting transfers between devices: 6.07 us -> none  [exchange(): return lax.all_to_all(array, axes, split_axis=0, concat_axis=0, tiled=True)]
    pallas_call x3 -> x2, Pallas kernels: 8.74 us -> 5.82 us  [apply_own(): pl.pallas_call(apply_own_kernel, in_specs=[SMEM] + [VMEM] * 2, out_specs=...]
    pallas_call x1, Pallas kernels: 0.85 us -> 3.72 us  [apply_own_hidden(): pl.pallas_call(apply_own_hidden_kernel, in_specs=[SMEM] + [VMEM] * 3, out...]
  transfers between devices with their start and end apart: 7 -> 6, of which waited for: 3 -> 2; matrix products, arithmetic and copies ran while one was open for 0% -> 0% of each run, Pallas kernels for 5% -> 5%
where the time goes in v4:
time: 185 us
  blocking collectives  145 us (78%)
  Pallas kernels  17.7 us (10%)
  starting transfers between devices  13.9 us (8%)
  local copies, waits for them, and re-layouts  3.36 us (2%)
  waiting for transfers between devices  2.17 us (1%)
    all_to_all x9, blocking collectives, exchange(): return lax.all_to_all(array, axes, split_axis=0, concat_axis=0, tiled=True)  145 us
    ppermute x3, starting transfers between devices, halo(): low = lax.ppermute(send_high, NODE, forward)  9.86 us
    pallas_call x2, Pallas kernels, apply_own(): pl.pallas_call(apply_own_kernel, in_specs=[SMEM] + [VMEM] * 2, out_specs=...  5.82 us
    ppermute x3, starting transfers between devices, halo(): high = lax.ppermute(send_low, NODE, backward)  4.01 us
    pallas_call x3, Pallas kernels, apply_halo(): pl.pallas_call(apply_halo_kernel, in_specs=[SMEM] + [VMEM] * 4, out_specs...  3.9 us
    pallas_call x1, Pallas kernels, apply_own_hidden(): pl.pallas_call(apply_own_hidden_kernel, in_specs=[SMEM] + [VMEM] * 3, out...  3.72 us
  transfers between devices with their start and end apart: 6, of which 2 were waited for; matrix products, arithmetic and copies ran while one was open for 0% of the time, Pallas kernels for 5%

profile of v4, /device:TPU:1, one launch (start us, length us, event | category | flops | bytes accessed | tf_op | source)
XLA Modules:
  0.0 184.7 jit_solution(3612630712991734872)
XLA Ops:
  1.4 0.7 add_add_fusion.slots
  2.2 0.9 copy-done.4
  3.1 0.9 split_blocks.1
  4.0 4.4 %collective-permute-start = (bf16[16,32,128]{2,1,0:T(8,128)(2,1)S(1)}, bf16[16,32,128]{2,1,0:T(8,128)(2,1)S(1)}, u32[]{:S(2)}, u32[]{:S(2)}) collective-permute-start(bf16[16,32,128]{2,1,0:T(8,128)(2,1)S(1)} %get-tuple-element.20), channel_id=1, source_target_pairs={{0,8},{8,16},{16,24},{24,32},{32,40},{40,48},{48,56},{56,64},{64,7... | collective-permute-start | bytes 393224 | tf_op jit(solution)/shard_map/ppermute | solution.py:46
  8.4 1.3 collective-permute-start.1
  9.7 2.2 %copy-done = bf16[128,128,128]{2,1,0:T(8,128)(2,1)S(1)} copy-done((bf16[128,128,128]{2,1,0:T(8,128)(2,1)S(1)}, bf16[128,128,128]{2,1,0:T(8,128)(2,1)}, u32[]{:S(2)}) %copy-start) | copy-done | bytes 4194328
  11.9 2.9 %apply_own.2.begun = f32[33,32,128]{2,1,0:T(8,128)S(1)} custom-call(s32[8,128]{1,0:T(8,128)S(1)} %get-tuple-element.18.tables, bf16[32,32,128]{2,1,0:T(8,128)(2,1)S(1)} %get-tuple-element.19.own, bf16[128,128,128]{2,1,0:T(8,128)(2,1)S(1)} %copy-done), custom_call_target="tpu_custom_call" | custom-call | tf_op jit(solution)/shard_map/apply_own/pallas_call | solution.py:163
  14.8 1.3 apply_halo.3
  16.1 20.4 %all_to_all.45.spread.spread_one = bf16[32,32,128]{2,1,0:T(8,128)(2,1)S(1)} all-to-all(bf16[32,32,128]{2,1,0:T(8,128)(2,1)S(1)} %apply_halo.3), channel_id=1, replica_groups=mesh['x'=4,'zhi'=8,'zlo'=4,'y'=4,'core'=2] {'y','core'}, dimensions={0} | all-to-all | bytes 524288 | tf_op jit(solution)/shard_map/all_to_all | solution.py:39
  36.5 0.4 mix_one.1
  36.9 9.9 %all_to_all.46.own.blocks = bf16[32,32,128]{2,1,0:T(8,128)(2,1)S(1)} all-to-all(bf16[32,32,128]{2,1,0:T(8,128)(2,1)S(1)} %get-tuple-element.22.hidden_one), channel_id=1, replica_groups=mesh['x'=4,'zhi'=8,'zlo'=4,'y'=4,'core'=2] {'y','core'}, dimensions={0} | all-to-all | bytes 524288 | tf_op jit(solution)/shard_map/all_to_all | solution.py:39
  46.9 0.6 sends_of.1
  47.5 3.8 %collective-permute-start.2 = (bf16[16,32,128]{2,1,0:T(8,128)(2,1)S(1)}, bf16[16,32,128]{2,1,0:T(8,128)(2,1)S(1)}, u32[]{:S(2)}, u32[]{:S(2)}) collective-permute-start(bf16[16,32,128]{2,1,0:T(8,128)(2,1)S(1)} %get-tuple-element.23), channel_id=1, source_target_pairs={{0,8},{8,16},{16,24},{24,32},{32,40},{40,48},{48,56},{56,64},{64,7... | collective-permute-start | bytes 393224 | tf_op jit(solution)/shard_map/ppermute | solution.py:46
  51.4 1.4 collective-permute-start.3
  52.8 2.9 %apply_own.3.begun = f32[33,32,128]{2,1,0:T(8,128)S(1)} custom-call(s32[8,128]{1,0:T(8,128)S(1)} %get-tuple-element.18.tables, bf16[32,32,128]{2,1,0:T(8,128)(2,1)S(1)} %all_to_all.46.own.blocks, bf16[128,128,128]{2,1,0:T(8,128)(2,1)S(1)} %copy-done.1), custom_call_target="tpu_custom_call" | custom-call | tf_op jit(solution)/shard_map/apply_own/pallas_call | solution.py:163
  55.7 1.5 collective-permute-done.3.high
  57.2 1.3 apply_halo.4
  58.5 11.4 %all_to_all.47.spread = bf16[32,32,128]{2,1,0:T(8,128)(2,1)S(1)} all-to-all(bf16[32,32,128]{2,1,0:T(8,128)(2,1)S(1)} %apply_halo.4), channel_id=1, replica_groups=mesh['x'=4,'zhi'=8,'zlo'=4,'y'=4,'core'=2] {'y','core'}, dimensions={0} | all-to-all | bytes 524288 | tf_op jit(solution)/shard_map/all_to_all | solution.py:39
  70.2 9.9 %all_to_all.48.pre_two = bf16[32,32,128]{2,1,0:T(8,128)(2,1)S(1)} all-to-all(bf16[32,32,128]{2,1,0:T(8,128)(2,1)S(1)} %mix_two.1), channel_id=1, replica_groups=mesh['x'=4,'zhi'=8,'zlo'=4,'y'=4,'core'=2] {'y','core'}, dimensions={0} | all-to-all | bytes 524288 | tf_op jit(solution)/shard_map/all_to_all | solution.py:39
  80.1 0.8 turn.1
  81.0 1.6 collective-permute-start.4
  82.6 1.3 collective-permute-start.5
  83.9 3.7 %apply_own_hidden.1 = (f32[33,32,128]{2,1,0:T(8,128)S(1)}, bf16[32,4096]{1,0:T(8,128)(2,1)}) custom-call(s32[8,128]{1,0:T(8,128)S(1)} %get-tuple-element.18.tables, bf16[32,32,128]{2,1,0:T(8,128)(2,1)S(1)} %get-tuple-element.25.own, bf16[128,128,128]{2,1,0:T(8,128)(2,1)S(1)} %copy-done.2, bf16[32,32,128]{2,1,0:T(8,128)(2,1)S(1)} %all_to_all.48.pre_two), custom_call_target="tpu_custom_call" | custom-call | tf_op jit(solution)/shard_map/apply_own_hidden/pallas_call | solution.py:287
  87.7 0.7 collective-permute-done.5.high
  88.3 1.3 apply_halo.5
  89.6 11.4 %all_to_all.49.back_two = bf16[32,32,128]{2,1,0:T(8,128)(2,1)S(1)} all-to-all(bf16[32,32,128]{2,1,0:T(8,128)(2,1)S(1)} %apply_halo.5), channel_id=1, replica_groups=mesh['x'=4,'zhi'=8,'zlo'=4,'y'=4,'core'=2] {'y','core'}, dimensions={0} | all-to-all | bytes 524288 | tf_op jit(solution)/shard_map/all_to_all | solution.py:39
  101.0 0.5 grads.1
  101.5 24.5 %all_to_all.50 = bf16[32,32,128]{2,1,0:T(8,128)(2,1)S(1)} all-to-all(bf16[32,32,128]{2,1,0:T(8,128)(2,1)S(1)} %grads.1), channel_id=1, replica_groups=mesh['x'=4,'zhi'=8,'zlo'=4,'y'=4,'core'=2] {'x','y','core'}, dimensions={0} | all-to-all | bytes 524288 | tf_op jit(solution)/shard_map/all_to_all | solution.py:39
  126.1 7.1 %all_to_all.51 = f32[4,32,128]{2,1,0:T(8,128)S(1)} all-to-all(f32[4,32,128]{2,1,0:T(8,128)S(1)} %broadcast_in_dim.12), channel_id=1, replica_groups=mesh['x'=4,'zhi'=8,'zlo'=4,'y'=4,'core'=2] {'zlo'}, dimensions={0} | all-to-all | bytes 131072 | tf_op jit(solution)/shard_map/all_to_all | solution.py:39
  133.2 36.0 %all_to_all.52 = bf16[8,32,128]{2,1,0:T(8,128)(2,1)S(1)} all-to-all(bf16[8,32,128]{2,1,0:T(8,128)(2,1)S(1)} %broadcast_in_dim.13), channel_id=1, replica_groups=mesh['x'=4,'zhi'=8,'zlo'=4,'y'=4,'core'=2] {'zhi'}, dimensions={0} | all-to-all | bytes 131072 | tf_op jit(solution)/shard_map/all_to_all | solution.py:39
  169.3 14.7 %all_to_all.53.pieces = bf16[32,32,128]{2,1,0:T(8,128)(2,1)S(1)} all-to-all(bf16[32,32,128]{2,1,0:T(8,128)(2,1)S(1)} %broadcast_in_dim.28), channel_id=1, replica_groups=mesh['x'=4,'zhi'=8,'zlo'=4,'y'=4,'core'=2] {'x','y','core'}, dimensions={0} | all-to-all | bytes 524288 | tf_op jit(solution)/shard_map/all_to_all | solution.py:39
  183.9 0.8 finish.1
  (25 shorter events, 0.6 us)
Async XLA Ops:
  2.2 0.9 copy-start.4
  4.0 10.8 %collective-permute-start = (bf16[16,32,128]{2,1,0:T(8,128)(2,1)S(1)}, bf16[16,32,128]{2,1,0:T(8,128)(2,1)S(1)}, u32[]{:S(2)}, u32[]{:S(2)}) collective-permute-start(bf16[16,32,128]{2,1,0:T(8,128)(2,1)S(1)} %get-tuple-element.20), channel_id=1, source_target_pairs={{0,8},{8,16},{16,24},{24,32},{32,40},{40,48},{48,56},{56,64},{64,7... | collective-permute-start | bytes 393224 | tf_op jit(solution)/shard_map/ppermute | solution.py:46
  8.4 6.4 %collective-permute-start.1 = (bf16[16,32,128]{2,1,0:T(8,128)(2,1)S(1)}, bf16[16,32,128]{2,1,0:T(8,128)(2,1)S(1)}, u32[]{:S(2)}, u32[]{:S(2)}) collective-permute-start(bf16[16,32,128]{2,1,0:T(8,128)(2,1)S(1)} %get-tuple-element.21), channel_id=1, source_target_pairs={{8,0},{16,8},{24,16},{32,24},{40,32},{48,40},{56,48},{64,56},{72,6... | collective-permute-start | bytes 393224 | tf_op jit(solution)/shard_map/ppermute | solution.py:47
  9.7 2.2 %copy-start = (bf16[128,128,128]{2,1,0:T(8,128)(2,1)S(1)}, bf16[128,128,128]{2,1,0:T(8,128)(2,1)}, u32[]{:S(2)}) copy-start(bf16[128,128,128]{2,1,0:T(8,128)(2,1)} %adj.9) | copy-start | bytes 12582916
  11.9 2.9 %copy-start.1 = (bf16[128,128,128]{2,1,0:T(8,128)(2,1)S(1)}, bf16[128,128,128]{2,1,0:T(8,128)(2,1)}, u32[]{:S(2)}) copy-start(bf16[128,128,128]{2,1,0:T(8,128)(2,1)} %adj.9) | copy-start | bytes 12582916
  11.9 24.7 %copy-start.6 = (bf16[256,256]{1,0:T(8,128)(2,1)S(1)}, bf16[256,256]{1,0:T(8,128)(2,1)}, u32[]{:S(2)}) copy-start(bf16[256,256]{1,0:T(8,128)(2,1)} %weight.3) | copy-start | bytes 393220
  47.5 8.2 %collective-permute-start.2 = (bf16[16,32,128]{2,1,0:T(8,128)(2,1)S(1)}, bf16[16,32,128]{2,1,0:T(8,128)(2,1)S(1)}, u32[]{:S(2)}, u32[]{:S(2)}) collective-permute-start(bf16[16,32,128]{2,1,0:T(8,128)(2,1)S(1)} %get-tuple-element.23), channel_id=1, source_target_pairs={{0,8},{8,16},{16,24},{24,32},{32,40},{40,48},{48,56},{56,64},{64,7... | collective-permute-start | bytes 393224 | tf_op jit(solution)/shard_map/ppermute | solution.py:46
  51.4 18.5 %copy-start.3 = (bf16[256,256]{1,0:T(8,128)(2,1)S(1)}, bf16[256,256]{1,0:T(8,128)(2,1)}, u32[]{:S(2)}) copy-start(bf16[256,256]{1,0:T(8,128)(2,1)} %weight.5) | copy-start | bytes 393220
  51.4 5.8 %collective-permute-start.3 = (bf16[16,32,128]{2,1,0:T(8,128)(2,1)S(1)}, bf16[16,32,128]{2,1,0:T(8,128)(2,1)S(1)}, u32[]{:S(2)}, u32[]{:S(2)}) collective-permute-start(bf16[16,32,128]{2,1,0:T(8,128)(2,1)S(1)} %get-tuple-element.24), channel_id=1, source_target_pairs={{8,0},{16,8},{24,16},{32,24},{40,32},{48,40},{56,48},{64,56},{72,6... | collective-permute-start | bytes 393224 | tf_op jit(solution)/shard_map/ppermute | solution.py:47
  55.7 24.4 %copy-start.5 = (bf16[32,4096]{1,0:T(8,128)(2,1)S(1)}, bf16[32,4096]{1,0:T(8,128)(2,1)}, u32[]{:S(2)}) copy-start(bf16[32,4096]{1,0:T(8,128)(2,1)} %cotangent.1) | copy-start | bytes 786436
  55.7 28.2 %copy-start.2 = (bf16[128,128,128]{2,1,0:T(8,128)(2,1)S(1)}, bf16[128,128,128]{2,1,0:T(8,128)(2,1)}, u32[]{:S(2)}) copy-start(bf16[128,128,128]{2,1,0:T(8,128)(2,1)} %adj.11) | copy-start | bytes 12582916
  81.0 6.7 %collective-permute-start.4 = (bf16[16,32,128]{2,1,0:T(8,128)(2,1)S(1)}, bf16[16,32,128]{2,1,0:T(8,128)(2,1)S(1)}, u32[]{:S(2)}, u32[]{:S(2)}) collective-permute-start(bf16[16,32,128]{2,1,0:T(8,128)(2,1)S(1)} %get-tuple-element.28), channel_id=1, source_target_pairs={{0,8},{8,16},{16,24},{24,32},{32,40},{40,48},{48,56},{56,64},{64,7... | collective-permute-start | bytes 393224 | tf_op jit(solution)/shard_map/ppermute | solution.py:46
  82.6 5.7 %collective-permute-start.5 = (bf16[16,32,128]{2,1,0:T(8,128)(2,1)S(1)}, bf16[16,32,128]{2,1,0:T(8,128)(2,1)S(1)}, u32[]{:S(2)}, u32[]{:S(2)}) collective-permute-start(bf16[16,32,128]{2,1,0:T(8,128)(2,1)S(1)} %get-tuple-element.29), channel_id=1, source_target_pairs={{8,0},{16,8},{24,16},{32,24},{40,32},{48,40},{56,48},{64,56},{72,6... | collective-permute-start | bytes 393224 | tf_op jit(solution)/shard_map/ppermute | solution.py:47

commit v5 on v4

--- a/solution.py
+++ b/solution.py
@@ -124,6 +124,7 @@
         ],
         scratch_shapes=[pltpu.SMEM((8, BLK), jnp.int32), pltpu.SemaphoreType.DMA],
         compiler_params=PARAMS,
+        cost_estimate=pl.CostEstimate(flops=2**32, bytes_accessed=2**20, transcendentals=0),
         name="split_blocks",
     )(slots, source)
 
@@ -356,8 +357,8 @@
 
 def sum_everywhere(partial):
     pieces = exchange(partial, PLANE).reshape(lax.axis_size(PLANE), -1, BLK)
-    piece = jnp.sum(pieces.astype(F32), axis=0)
-    piece = jnp.sum(gather_pieces(piece, "zlo"), axis=0).astype(BF16)
+    piece = jnp.sum(pieces.astype(F32), axis=0).astype(BF16)
+    piece = jnp.sum(gather_pieces(piece, "zlo").astype(F32), axis=0).astype(BF16)
     piece = jnp.sum(gather_pieces(piece, "zhi").astype(F32), axis=0).astype(BF16)
     return gather_pieces(piece, PLANE).reshape(partial.shape)
 

time: 185 us -> 183 us (0.989)
  local copies, waits for them, and re-layouts: 3.36 us -> 1.18 us
  starting transfers between devices: 13.9 us -> 11.9 us
    unnamed x14 -> x12, local copies, waits for them, and re-layouts: 3.16 us -> 0.98 us
    ppermute x3, starting transfers between devices: 9.86 us -> 7.85 us  [halo(): low = lax.ppermute(send_high, NODE, forward)]
  transfers between devices with their start and end apart: 6 -> 6, of which waited for: 2 -> 3; matrix products, arithmetic and copies ran while one was open for 0% -> 0% of each run, Pallas kernels for 5% -> 5%
where the time goes in v5:
time: 183 us; the launch traced here: 182 us
  blocking collectives  145 us (79%)
  Pallas kernels  17.7 us (10%)
  starting transfers between devices  11.9 us (7%)
  waiting for transfers between devices  3.83 us (2%)
    all_to_all x9, blocking collectives, exchange(): return lax.all_to_all(array, axes, split_axis=0, concat_axis=0, tiled=True)  145 us
    ppermute x3, starting transfers between devices, halo(): low = lax.ppermute(send_high, NODE, forward)  7.85 us
    pallas_call x2, Pallas kernels, apply_own(): pl.pallas_call(apply_own_kernel, in_specs=[SMEM] + [VMEM] * 2, out_specs=...  5.81 us
    ppermute x3, starting transfers between devices, halo(): high = lax.ppermute(send_low, NODE, backward)  4.01 us
    pallas_call x3, Pallas kernels, apply_halo(): pl.pallas_call(apply_halo_kernel, in_specs=[SMEM] + [VMEM] * 4, out_specs...  3.9 us
    ppermute x3, waiting for transfers between devices, halo(): high = lax.ppermute(send_low, NODE, backward)  3.81 us
    pallas_call x1, Pallas kernels, apply_own_hidden(): pl.pallas_call(apply_own_hidden_kernel, in_specs=[SMEM] + [VMEM] * 3, out...  3.71 us
  transfers between devices with their start and end apart: 6, of which 3 were waited for; matrix products, arithmetic and copies ran while one was open for 0% of the time, Pallas kernels for 5%

profile of v5, /device:TPU:1, one launch (start us, length us, event | category | flops | bytes accessed | tf_op | source)
XLA Modules:
  0.0 182.2 jit_solution(11079048453404440292)
XLA Ops:
  1.4 0.7 add_add_fusion.slots
  2.2 0.9 copy-done.5
  3.1 0.9 split_blocks.1
  4.0 4.5 %collective-permute-start = (bf16[16,32,128]{2,1,0:T(8,128)(2,1)S(1)}, bf16[16,32,128]{2,1,0:T(8,128)(2,1)S(1)}, u32[]{:S(2)}, u32[]{:S(2)}) collective-permute-start(bf16[16,32,128]{2,1,0:T(8,128)(2,1)S(1)} %get-tuple-element.20), channel_id=1, source_target_pairs={{0,8},{8,16},{16,24},{24,32},{32,40},{40,48},{48,56},{56,64},{64,7... | collective-permute-start | bytes 393224 | tf_op jit(solution)/shard_map/ppermute | solution.py:46
  8.5 1.3 collective-permute-start.1
  9.8 2.9 %apply_own.2.begun = f32[33,32,128]{2,1,0:T(8,128)S(1)} custom-call(s32[8,128]{1,0:T(8,128)S(1)} %get-tuple-element.18.tables, bf16[32,32,128]{2,1,0:T(8,128)(2,1)S(1)} %get-tuple-element.19.own, bf16[128,128,128]{2,1,0:T(8,128)(2,1)S(1)} %copy-done), custom_call_target="tpu_custom_call" | custom-call | tf_op jit(solution)/shard_map/apply_own/pallas_call | solution.py:164
  12.8 1.6 collective-permute-done.1.high
  14.4 1.3 apply_halo.3
  15.7 20.9 %all_to_all.45.spread.spread_one = bf16[32,32,128]{2,1,0:T(8,128)(2,1)S(1)} all-to-all(bf16[32,32,128]{2,1,0:T(8,128)(2,1)S(1)} %apply_halo.3), channel_id=1, replica_groups=mesh['x'=4,'zhi'=8,'zlo'=4,'y'=4,'core'=2] {'y','core'}, dimensions={0} | all-to-all | bytes 524288 | tf_op jit(solution)/shard_map/all_to_all | solution.py:39
  36.7 0.4 mix_one.1
  37.1 9.9 %all_to_all.46.own.blocks = bf16[32,32,128]{2,1,0:T(8,128)(2,1)S(1)} all-to-all(bf16[32,32,128]{2,1,0:T(8,128)(2,1)S(1)} %get-tuple-element.22.hidden_one), channel_id=1, replica_groups=mesh['x'=4,'zhi'=8,'zlo'=4,'y'=4,'core'=2] {'y','core'}, dimensions={0} | all-to-all | bytes 524288 | tf_op jit(solution)/shard_map/all_to_all | solution.py:39
  47.0 0.6 sends_of.1
  47.7 1.7 collective-permute-start.2
  49.4 1.4 collective-permute-start.3
  50.8 2.9 %apply_own.3.begun = f32[33,32,128]{2,1,0:T(8,128)S(1)} custom-call(s32[8,128]{1,0:T(8,128)S(1)} %get-tuple-element.18.tables, bf16[32,32,128]{2,1,0:T(8,128)(2,1)S(1)} %all_to_all.46.own.blocks, bf16[128,128,128]{2,1,0:T(8,128)(2,1)S(1)} %copy-done), custom_call_target="tpu_custom_call" | custom-call | tf_op jit(solution)/shard_map/apply_own/pallas_call | solution.py:164
  53.7 1.5 collective-permute-done.3.high
  55.2 1.3 apply_halo.4
  56.5 11.4 %all_to_all.47.spread = bf16[32,32,128]{2,1,0:T(8,128)(2,1)S(1)} all-to-all(bf16[32,32,128]{2,1,0:T(8,128)(2,1)S(1)} %apply_halo.4), channel_id=1, replica_groups=mesh['x'=4,'zhi'=8,'zlo'=4,'y'=4,'core'=2] {'y','core'}, dimensions={0} | all-to-all | bytes 524288 | tf_op jit(solution)/shard_map/all_to_all | solution.py:39
  68.1 9.9 %all_to_all.48.pre_two = bf16[32,32,128]{2,1,0:T(8,128)(2,1)S(1)} all-to-all(bf16[32,32,128]{2,1,0:T(8,128)(2,1)S(1)} %mix_two.1), channel_id=1, replica_groups=mesh['x'=4,'zhi'=8,'zlo'=4,'y'=4,'core'=2] {'y','core'}, dimensions={0} | all-to-all | bytes 524288 | tf_op jit(solution)/shard_map/all_to_all | solution.py:39
  78.1 0.8 turn.1
  78.9 1.7 collective-permute-start.4
  80.6 1.3 collective-permute-start.5
  81.9 3.7 %apply_own_hidden.1 = (f32[33,32,128]{2,1,0:T(8,128)S(1)}, bf16[32,4096]{1,0:T(8,128)(2,1)}) custom-call(s32[8,128]{1,0:T(8,128)S(1)} %get-tuple-element.18.tables, bf16[32,32,128]{2,1,0:T(8,128)(2,1)S(1)} %get-tuple-element.25.own, bf16[128,128,128]{2,1,0:T(8,128)(2,1)S(1)} %copy-done.1, bf16[32,32,128]{2,1,0:T(8,128)(2,1)S(1)} %all_to_all.48.pre_two), custom_call_target="tpu_custom_call" | custom-call | tf_op jit(solution)/shard_map/apply_own_hidden/pallas_call | solution.py:288
  85.6 0.7 collective-permute-done.5.high
  86.3 1.3 apply_halo.5
  87.6 11.4 %all_to_all.49.back_two = bf16[32,32,128]{2,1,0:T(8,128)(2,1)S(1)} all-to-all(bf16[32,32,128]{2,1,0:T(8,128)(2,1)S(1)} %apply_halo.5), channel_id=1, replica_groups=mesh['x'=4,'zhi'=8,'zlo'=4,'y'=4,'core'=2] {'y','core'}, dimensions={0} | all-to-all | bytes 524288 | tf_op jit(solution)/shard_map/all_to_all | solution.py:39
  99.0 0.5 grads.1
  99.5 24.8 %all_to_all.50 = bf16[32,32,128]{2,1,0:T(8,128)(2,1)S(1)} all-to-all(bf16[32,32,128]{2,1,0:T(8,128)(2,1)S(1)} %grads.1), channel_id=1, replica_groups=mesh['x'=4,'zhi'=8,'zlo'=4,'y'=4,'core'=2] {'x','y','core'}, dimensions={0} | all-to-all | bytes 524288 | tf_op jit(solution)/shard_map/all_to_all | solution.py:39
  124.3 6.9 %all_to_all.51 = bf16[4,32,128]{2,1,0:T(8,128)(2,1)S(1)} all-to-all(bf16[4,32,128]{2,1,0:T(8,128)(2,1)S(1)} %broadcast_in_dim.12), channel_id=1, replica_groups=mesh['x'=4,'zhi'=8,'zlo'=4,'y'=4,'core'=2] {'zlo'}, dimensions={0} | all-to-all | bytes 65536 | tf_op jit(solution)/shard_map/all_to_all | solution.py:39
  131.2 35.8 %all_to_all.52 = bf16[8,32,128]{2,1,0:T(8,128)(2,1)S(1)} all-to-all(bf16[8,32,128]{2,1,0:T(8,128)(2,1)S(1)} %broadcast_in_dim.13), channel_id=1, replica_groups=mesh['x'=4,'zhi'=8,'zlo'=4,'y'=4,'core'=2] {'zhi'}, dimensions={0} | all-to-all | bytes 131072 | tf_op jit(solution)/shard_map/all_to_all | solution.py:39
  167.0 14.3 %all_to_all.53.pieces = bf16[32,32,128]{2,1,0:T(8,128)(2,1)S(1)} all-to-all(bf16[32,32,128]{2,1,0:T(8,128)(2,1)S(1)} %broadcast_in_dim.28), channel_id=1, replica_groups=mesh['x'=4,'zhi'=8,'zlo'=4,'y'=4,'core'=2] {'x','y','core'}, dimensions={0} | all-to-all | bytes 524288 | tf_op jit(solution)/shard_map/all_to_all | solution.py:39
  181.4 0.8 finish.1
  (23 shorter events, 0.6 us)
Async XLA Ops:
  2.2 0.9 copy-start.5
  3.1 6.7 %copy-start = (bf16[128,128,128]{2,1,0:T(8,128)(2,1)S(1)}, bf16[128,128,128]{2,1,0:T(8,128)(2,1)}, u32[]{:S(2)}) copy-start(bf16[128,128,128]{2,1,0:T(8,128)(2,1)} %adj.9) | copy-start | bytes 12582916
  4.0 8.8 %collective-permute-start = (bf16[16,32,128]{2,1,0:T(8,128)(2,1)S(1)}, bf16[16,32,128]{2,1,0:T(8,128)(2,1)S(1)}, u32[]{:S(2)}, u32[]{:S(2)}) collective-permute-start(bf16[16,32,128]{2,1,0:T(8,128)(2,1)S(1)} %get-tuple-element.20), channel_id=1, source_target_pairs={{0,8},{8,16},{16,24},{24,32},{32,40},{40,48},{48,56},{56,64},{64,7... | collective-permute-start | bytes 393224 | tf_op jit(solution)/shard_map/ppermute | solution.py:46
  8.5 5.9 %collective-permute-start.1 = (bf16[16,32,128]{2,1,0:T(8,128)(2,1)S(1)}, bf16[16,32,128]{2,1,0:T(8,128)(2,1)S(1)}, u32[]{:S(2)}, u32[]{:S(2)}) collective-permute-start(bf16[16,32,128]{2,1,0:T(8,128)(2,1)S(1)} %get-tuple-element.21), channel_id=1, source_target_pairs={{8,0},{16,8},{24,16},{32,24},{40,32},{48,40},{56,48},{64,56},{72,6... | collective-permute-start | bytes 393224 | tf_op jit(solution)/shard_map/ppermute | solution.py:47
  9.8 26.8 %copy-start.4 = (bf16[256,256]{1,0:T(8,128)(2,1)S(1)}, bf16[256,256]{1,0:T(8,128)(2,1)}, u32[]{:S(2)}) copy-start(bf16[256,256]{1,0:T(8,128)(2,1)} %weight.3) | copy-start | bytes 393220
  47.7 6.1 %collective-permute-start.2 = (bf16[16,32,128]{2,1,0:T(8,128)(2,1)S(1)}, bf16[16,32,128]{2,1,0:T(8,128)(2,1)S(1)}, u32[]{:S(2)}, u32[]{:S(2)}) collective-permute-start(bf16[16,32,128]{2,1,0:T(8,128)(2,1)S(1)} %get-tuple-element.23), channel_id=1, source_target_pairs={{0,8},{8,16},{16,24},{24,32},{32,40},{40,48},{48,56},{56,64},{64,7... | collective-permute-start | bytes 393224 | tf_op jit(solution)/shard_map/ppermute | solution.py:46
  49.3 18.5 %copy-start.2 = (bf16[256,256]{1,0:T(8,128)(2,1)S(1)}, bf16[256,256]{1,0:T(8,128)(2,1)}, u32[]{:S(2)}) copy-start(bf16[256,256]{1,0:T(8,128)(2,1)} %weight.5) | copy-start | bytes 393220
  49.4 5.8 %collective-permute-start.3 = (bf16[16,32,128]{2,1,0:T(8,128)(2,1)S(1)}, bf16[16,32,128]{2,1,0:T(8,128)(2,1)S(1)}, u32[]{:S(2)}, u32[]{:S(2)}) collective-permute-start(bf16[16,32,128]{2,1,0:T(8,128)(2,1)S(1)} %get-tuple-element.24), channel_id=1, source_target_pairs={{8,0},{16,8},{24,16},{32,24},{40,32},{48,40},{56,48},{64,56},{72,6... | collective-permute-start | bytes 393224 | tf_op jit(solution)/shard_map/ppermute | solution.py:47
  53.7 24.4 %copy-start.3 = (bf16[32,4096]{1,0:T(8,128)(2,1)S(1)}, bf16[32,4096]{1,0:T(8,128)(2,1)}, u32[]{:S(2)}) copy-start(bf16[32,4096]{1,0:T(8,128)(2,1)} %cotangent.1) | copy-start | bytes 786436
  53.7 28.2 %copy-start.1 = (bf16[128,128,128]{2,1,0:T(8,128)(2,1)S(1)}, bf16[128,128,128]{2,1,0:T(8,128)(2,1)}, u32[]{:S(2)}) copy-start(bf16[128,128,128]{2,1,0:T(8,128)(2,1)} %adj.11) | copy-start | bytes 12582916
  78.9 6.7 %collective-permute-start.4 = (bf16[16,32,128]{2,1,0:T(8,128)(2,1)S(1)}, bf16[16,32,128]{2,1,0:T(8,128)(2,1)S(1)}, u32[]{:S(2)}, u32[]{:S(2)}) collective-permute-start(bf16[16,32,128]{2,1,0:T(8,128)(2,1)S(1)} %get-tuple-element.28), channel_id=1, source_target_pairs={{0,8},{8,16},{16,24},{24,32},{32,40},{40,48},{48,56},{56,64},{64,7... | collective-permute-start | bytes 393224 | tf_op jit(solution)/shard_map/ppermute | solution.py:46
  80.6 5.7 %collective-permute-start.5 = (bf16[16,32,128]{2,1,0:T(8,128)(2,1)S(1)}, bf16[16,32,128]{2,1,0:T(8,128)(2,1)S(1)}, u32[]{:S(2)}, u32[]{:S(2)}) collective-permute-start(bf16[16,32,128]{2,1,0:T(8,128)(2,1)S(1)} %get-tuple-element.29), channel_id=1, source_target_pairs={{8,0},{16,8},{24,16},{32,24},{40,32},{48,40},{56,48},{64,56},{72,6... | collective-permute-start | bytes 393224 | tf_op jit(solution)/shard_map/ppermute | solution.py:47

commit v6 on v5

--- a/solution.py
+++ b/solution.py
@@ -84,6 +84,8 @@
         jnp.where(own, rows, float(NBD)),
         total(received, slots),
         NBD + total(received, rows_down - NBD),
+        jnp.where(own, rows, 0.0),
+        jnp.where(own, local, float(NBD)),
     )
     return [table.astype(jnp.int32) for table in found]
 
@@ -144,9 +146,10 @@
     )(tables, blocks)
 
 
-def add_slots(total, batch):
+def add_slots(total, batch, adj_axis=1):
+    along = (((1,), (adj_axis,)), ((), ()))
     parts = [
-        lax.dot_general(block, adj, (((1,), (1,)), ((), ())), preferred_element_type=F32)
+        lax.dot_general(block, adj, along, preferred_element_type=F32)
         for block, adj, _ in batch
     ]
     for part, (_, _, row) in zip(parts, batch):
@@ -277,16 +280,19 @@
     )(tables, pre_two, cotangent)
 
 
-def apply_own_hidden_kernel(tables, own, adj, pre_two, total, hidden_out):
-    apply_own_kernel(tables, own, adj, total)
+def push_own_hidden_kernel(tables, own, adj, pre_two, total, hidden_out):
+    total[...] = jnp.zeros_like(total)
+    for start in range(0, adj.shape[0], BATCH):
+        slots = range(start, start + BATCH)
+        add_slots(total, [(own[tables[5, m]], adj[m], tables[6, m]) for m in slots], 0)
     for b in range(NBD):
         pre = pre_two[b].astype(F32)
         hidden_out[:, b * BLK : (b + 1) * BLK] = (pre * sigmoid(pre)).astype(BF16)
 
 
-def apply_own_hidden(tables, own, adj, pre_two):
-    return pl.pallas_call(
-        apply_own_hidden_kernel,
+def push_own_hidden(tables, own, adj, pre_two):
+    return pl.pallas_call(
+        push_own_hidden_kernel,
         in_specs=[SMEM] + [VMEM] * 3,
         out_specs=[VMEM] * 2,
         out_shape=[
@@ -294,7 +300,7 @@
             jax.ShapeDtypeStruct((FEATS, NBD * BLK), BF16),
         ],
         compiler_params=PARAMS,
-        name="apply_own_hidden",
+        name="push_own_hidden",
     )(tables, own, adj, pre_two)
 
 
@@ -385,7 +391,7 @@
     pre_two = exchange(mix_two(spread_two, weight_two), FEAT)
     delta_two, *sends = turn(tables, pre_two, cotangent)
     low, high = halo(*sends)
-    begun, hidden_out = apply_own_hidden(tables, delta_two, adj_tvalues, pre_two)
+    begun, hidden_out = push_own_hidden(tables, delta_two, adj_values, pre_two)
     back_two = exchange(apply_halo(tables, begun, low, high, adj_tvalues), FEAT)
     partial = grads(back_two, spread_one, hidden_rows, slope_one, weight_two)
     grad_one, grad_two = finish(sum_everywhere(partial))

time: 183 us -> 183 us (level)
  no operation moved by 1% of the time
where the time goes in v6:
time: 183 us; the launch traced here: 182 us
  blocking collectives  146 us (80%)
  Pallas kernels  16.6 us (9%)
  starting transfers between devices  11.8 us (6%)
  waiting for transfers between devices  4.93 us (3%)
    all_to_all x9, blocking collectives, exchange(): return lax.all_to_all(array, axes, split_axis=0, concat_axis=0, tiled=True)  146 us
    ppermute x3, starting transfers between devices, halo(): low = lax.ppermute(send_high, NODE, forward)  7.81 us
    pallas_call x2, Pallas kernels, apply_own(): pl.pallas_call(apply_own_kernel, in_specs=[SMEM] + [VMEM] * 2, out_specs=...  5.81 us
    ppermute x3, waiting for transfers between devices, halo(): high = lax.ppermute(send_low, NODE, backward)  4.91 us
    ppermute x3, starting transfers between devices, halo(): high = lax.ppermute(send_low, NODE, backward)  4.01 us
    pallas_call x3, Pallas kernels, apply_halo(): pl.pallas_call(apply_halo_kernel, in_specs=[SMEM] + [VMEM] * 4, out_specs...  3.9 us
  transfers between devices with their start and end apart: 6, of which 3 were waited for; matrix products, arithmetic and copies ran while one was open for 0% of the time, Pallas kernels for 5%

profile of v6, /device:TPU:1, one launch (start us, length us, event | category | flops | bytes accessed | tf_op | source)
XLA Modules:
  0.0 182.4 jit_solution(8515165026093645263)
XLA Ops:
  1.4 0.7 add_add_fusion.slots
  2.2 0.9 copy-done.5
  3.1 0.9 split_blocks.1
  4.0 4.5 %collective-permute-start = (bf16[16,32,128]{2,1,0:T(8,128)(2,1)S(1)}, bf16[16,32,128]{2,1,0:T(8,128)(2,1)S(1)}, u32[]{:S(2)}, u32[]{:S(2)}) collective-permute-start(bf16[16,32,128]{2,1,0:T(8,128)(2,1)S(1)} %get-tuple-element.20), channel_id=1, source_target_pairs={{0,8},{8,16},{16,24},{24,32},{32,40},{40,48},{48,56},{56,64},{64,7... | collective-permute-start | bytes 393224 | tf_op jit(solution)/shard_map/ppermute | solution.py:46
  8.5 1.3 collective-permute-start.1
  9.8 2.9 %apply_own.2.begun = f32[33,32,128]{2,1,0:T(8,128)S(1)} custom-call(s32[8,128]{1,0:T(8,128)S(1)} %get-tuple-element.18.tables, bf16[32,32,128]{2,1,0:T(8,128)(2,1)S(1)} %get-tuple-element.19.own, bf16[128,128,128]{2,1,0:T(8,128)(2,1)S(1)} %copy-done), custom_call_target="tpu_custom_call" | custom-call | tf_op jit(solution)/shard_map/apply_own/pallas_call | solution.py:167
  12.8 1.6 collective-permute-done.1.high
  14.4 1.3 apply_halo.3
  15.7 20.9 %all_to_all.45.spread.spread_one = bf16[32,32,128]{2,1,0:T(8,128)(2,1)S(1)} all-to-all(bf16[32,32,128]{2,1,0:T(8,128)(2,1)S(1)} %apply_halo.3), channel_id=1, replica_groups=mesh['x'=4,'zhi'=8,'zlo'=4,'y'=4,'core'=2] {'y','core'}, dimensions={0} | all-to-all | bytes 524288 | tf_op jit(solution)/shard_map/all_to_all | solution.py:39
  36.7 0.4 mix_one.1
  37.1 9.9 %all_to_all.46.own.blocks = bf16[32,32,128]{2,1,0:T(8,128)(2,1)S(1)} all-to-all(bf16[32,32,128]{2,1,0:T(8,128)(2,1)S(1)} %get-tuple-element.22.hidden_one), channel_id=1, replica_groups=mesh['x'=4,'zhi'=8,'zlo'=4,'y'=4,'core'=2] {'y','core'}, dimensions={0} | all-to-all | bytes 524288 | tf_op jit(solution)/shard_map/all_to_all | solution.py:39
  47.0 0.6 sends_of.1
  47.7 1.7 collective-permute-start.2
  49.3 1.4 collective-permute-start.3
  50.8 2.9 %apply_own.3.begun = f32[33,32,128]{2,1,0:T(8,128)S(1)} custom-call(s32[8,128]{1,0:T(8,128)S(1)} %get-tuple-element.18.tables, bf16[32,32,128]{2,1,0:T(8,128)(2,1)S(1)} %all_to_all.46.own.blocks, bf16[128,128,128]{2,1,0:T(8,128)(2,1)S(1)} %copy-done), custom_call_target="tpu_custom_call" | custom-call | tf_op jit(solution)/shard_map/apply_own/pallas_call | solution.py:167
  53.7 1.5 collective-permute-done.3.high
  55.2 1.3 apply_halo.4
  56.5 11.6 %all_to_all.47.spread = bf16[32,32,128]{2,1,0:T(8,128)(2,1)S(1)} all-to-all(bf16[32,32,128]{2,1,0:T(8,128)(2,1)S(1)} %apply_halo.4), channel_id=1, replica_groups=mesh['x'=4,'zhi'=8,'zlo'=4,'y'=4,'core'=2] {'y','core'}, dimensions={0} | all-to-all | bytes 524288 | tf_op jit(solution)/shard_map/all_to_all | solution.py:39
  68.4 9.9 %all_to_all.48.pre_two = bf16[32,32,128]{2,1,0:T(8,128)(2,1)S(1)} all-to-all(bf16[32,32,128]{2,1,0:T(8,128)(2,1)S(1)} %mix_two.1), channel_id=1, replica_groups=mesh['x'=4,'zhi'=8,'zlo'=4,'y'=4,'core'=2] {'y','core'}, dimensions={0} | all-to-all | bytes 524288 | tf_op jit(solution)/shard_map/all_to_all | solution.py:39
  78.3 0.8 turn.1
  79.2 1.6 collective-permute-start.4
  80.8 1.3 collective-permute-start.5
  82.1 2.6 %push_own_hidden.1 = (f32[33,32,128]{2,1,0:T(8,128)S(1)}, bf16[32,4096]{1,0:T(8,128)(2,1)}) custom-call(s32[8,128]{1,0:T(8,128)S(1)} %get-tuple-element.18.tables, bf16[32,32,128]{2,1,0:T(8,128)(2,1)S(1)} %get-tuple-element.25.own, bf16[128,128,128]{2,1,0:T(8,128)(2,1)S(1)} %copy-done, bf16[32,32,128]{2,1,0:T(8,128)(2,1)S(1)} %all_to_all.48.pre_two), custom_call_target="tpu_custom_call" | custom-call | tf_op jit(solution)/shard_map/push_own_hidden/pallas_call | solution.py:294
  84.8 1.8 collective-permute-done.5.high
  86.6 1.3 apply_halo.5
  87.9 11.4 %all_to_all.49.back_two = bf16[32,32,128]{2,1,0:T(8,128)(2,1)S(1)} all-to-all(bf16[32,32,128]{2,1,0:T(8,128)(2,1)S(1)} %apply_halo.5), channel_id=1, replica_groups=mesh['x'=4,'zhi'=8,'zlo'=4,'y'=4,'core'=2] {'y','core'}, dimensions={0} | all-to-all | bytes 524288 | tf_op jit(solution)/shard_map/all_to_all | solution.py:39
  99.2 0.5 grads.1
  99.7 23.7 %all_to_all.50 = bf16[32,32,128]{2,1,0:T(8,128)(2,1)S(1)} all-to-all(bf16[32,32,128]{2,1,0:T(8,128)(2,1)S(1)} %grads.1), channel_id=1, replica_groups=mesh['x'=4,'zhi'=8,'zlo'=4,'y'=4,'core'=2] {'x','y','core'}, dimensions={0} | all-to-all | bytes 524288 | tf_op jit(solution)/shard_map/all_to_all | solution.py:39
  123.5 6.9 %all_to_all.51 = bf16[4,32,128]{2,1,0:T(8,128)(2,1)S(1)} all-to-all(bf16[4,32,128]{2,1,0:T(8,128)(2,1)S(1)} %broadcast_in_dim.12), channel_id=1, replica_groups=mesh['x'=4,'zhi'=8,'zlo'=4,'y'=4,'core'=2] {'zlo'}, dimensions={0} | all-to-all | bytes 65536 | tf_op jit(solution)/shard_map/all_to_all | solution.py:39
  130.4 36.9 %all_to_all.52 = bf16[8,32,128]{2,1,0:T(8,128)(2,1)S(1)} all-to-all(bf16[8,32,128]{2,1,0:T(8,128)(2,1)S(1)} %broadcast_in_dim.13), channel_id=1, replica_groups=mesh['x'=4,'zhi'=8,'zlo'=4,'y'=4,'core'=2] {'zhi'}, dimensions={0} | all-to-all | bytes 131072 | tf_op jit(solution)/shard_map/all_to_all | solution.py:39
  167.3 14.3 %all_to_all.53.pieces = bf16[32,32,128]{2,1,0:T(8,128)(2,1)S(1)} all-to-all(bf16[32,32,128]{2,1,0:T(8,128)(2,1)S(1)} %broadcast_in_dim.28), channel_id=1, replica_groups=mesh['x'=4,'zhi'=8,'zlo'=4,'y'=4,'core'=2] {'x','y','core'}, dimensions={0} | all-to-all | bytes 524288 | tf_op jit(solution)/shard_map/all_to_all | solution.py:39
  181.6 0.8 finish.1
  (23 shorter events, 0.6 us)
Async XLA Ops:
  2.2 0.9 copy-start.5
  3.1 6.7 %copy-start = (bf16[128,128,128]{2,1,0:T(8,128)(2,1)S(1)}, bf16[128,128,128]{2,1,0:T(8,128)(2,1)}, u32[]{:S(2)}) copy-start(bf16[128,128,128]{2,1,0:T(8,128)(2,1)} %adj.10) | copy-start | bytes 12582916
  4.0 8.8 %collective-permute-start = (bf16[16,32,128]{2,1,0:T(8,128)(2,1)S(1)}, bf16[16,32,128]{2,1,0:T(8,128)(2,1)S(1)}, u32[]{:S(2)}, u32[]{:S(2)}) collective-permute-start(bf16[16,32,128]{2,1,0:T(8,128)(2,1)S(1)} %get-tuple-element.20), channel_id=1, source_target_pairs={{0,8},{8,16},{16,24},{24,32},{32,40},{40,48},{48,56},{56,64},{64,7... | collective-permute-start | bytes 393224 | tf_op jit(solution)/shard_map/ppermute | solution.py:46
  8.5 5.9 %collective-permute-start.1 = (bf16[16,32,128]{2,1,0:T(8,128)(2,1)S(1)}, bf16[16,32,128]{2,1,0:T(8,128)(2,1)S(1)}, u32[]{:S(2)}, u32[]{:S(2)}) collective-permute-start(bf16[16,32,128]{2,1,0:T(8,128)(2,1)S(1)} %get-tuple-element.21), channel_id=1, source_target_pairs={{8,0},{16,8},{24,16},{32,24},{40,32},{48,40},{56,48},{64,56},{72,6... | collective-permute-start | bytes 393224 | tf_op jit(solution)/shard_map/ppermute | solution.py:47
  9.8 26.8 %copy-start.4 = (bf16[256,256]{1,0:T(8,128)(2,1)S(1)}, bf16[256,256]{1,0:T(8,128)(2,1)}, u32[]{:S(2)}) copy-start(bf16[256,256]{1,0:T(8,128)(2,1)} %weight.3) | copy-start | bytes 393220
  47.7 6.0 %collective-permute-start.2 = (bf16[16,32,128]{2,1,0:T(8,128)(2,1)S(1)}, bf16[16,32,128]{2,1,0:T(8,128)(2,1)S(1)}, u32[]{:S(2)}, u32[]{:S(2)}) collective-permute-start(bf16[16,32,128]{2,1,0:T(8,128)(2,1)S(1)} %get-tuple-element.23), channel_id=1, source_target_pairs={{0,8},{8,16},{16,24},{24,32},{32,40},{40,48},{48,56},{56,64},{64,7... | collective-permute-start | bytes 393224 | tf_op jit(solution)/shard_map/ppermute | solution.py:46
  49.3 18.8 %copy-start.2 = (bf16[256,256]{1,0:T(8,128)(2,1)S(1)}, bf16[256,256]{1,0:T(8,128)(2,1)}, u32[]{:S(2)}) copy-start(bf16[256,256]{1,0:T(8,128)(2,1)} %weight.5) | copy-start | bytes 393220
  49.3 5.8 %collective-permute-start.3 = (bf16[16,32,128]{2,1,0:T(8,128)(2,1)S(1)}, bf16[16,32,128]{2,1,0:T(8,128)(2,1)S(1)}, u32[]{:S(2)}, u32[]{:S(2)}) collective-permute-start(bf16[16,32,128]{2,1,0:T(8,128)(2,1)S(1)} %get-tuple-element.24), channel_id=1, source_target_pairs={{8,0},{16,8},{24,16},{32,24},{40,32},{48,40},{56,48},{64,56},{72,6... | collective-permute-start | bytes 393224 | tf_op jit(solution)/shard_map/ppermute | solution.py:47
  53.7 24.7 %copy-start.3 = (bf16[32,4096]{1,0:T(8,128)(2,1)S(1)}, bf16[32,4096]{1,0:T(8,128)(2,1)}, u32[]{:S(2)}) copy-start(bf16[32,4096]{1,0:T(8,128)(2,1)} %cotangent.1) | copy-start | bytes 786436
  56.5 30.1 %copy-start.1 = (bf16[128,128,128]{2,1,0:T(8,128)(2,1)S(1)}, bf16[128,128,128]{2,1,0:T(8,128)(2,1)}, u32[]{:S(2)}) copy-start(bf16[128,128,128]{2,1,0:T(8,128)(2,1)} %adj.11) | copy-start | bytes 12582916
  79.2 5.6 %collective-permute-start.4 = (bf16[16,32,128]{2,1,0:T(8,128)(2,1)S(1)}, bf16[16,32,128]{2,1,0:T(8,128)(2,1)S(1)}, u32[]{:S(2)}, u32[]{:S(2)}) collective-permute-start(bf16[16,32,128]{2,1,0:T(8,128)(2,1)S(1)} %get-tuple-element.28), channel_id=1, source_target_pairs={{0,8},{8,16},{16,24},{24,32},{32,40},{40,48},{48,56},{56,64},{64,7... | collective-permute-start | bytes 393224 | tf_op jit(solution)/shard_map/ppermute | solution.py:46
  80.8 5.7 %collective-permute-start.5 = (bf16[16,32,128]{2,1,0:T(8,128)(2,1)S(1)}, bf16[16,32,128]{2,1,0:T(8,128)(2,1)S(1)}, u32[]{:S(2)}, u32[]{:S(2)}) collective-permute-start(bf16[16,32,128]{2,1,0:T(8,128)(2,1)S(1)} %get-tuple-element.29), channel_id=1, source_target_pairs={{8,0},{16,8},{24,16},{32,24},{40,32},{48,40},{56,48},{64,56},{72,6... | collective-permute-start | bytes 393224 | tf_op jit(solution)/shard_map/ppermute | solution.py:47

commit v7 on v6

--- a/solution.py
+++ b/solution.py
@@ -174,28 +174,45 @@
     )(tables, own, adj)
 
 
-def apply_halo_kernel(tables, begun, low, high, adj, out, total):
+def add_side(tables, total, blocks, adj, side):
+    for start in range(0, HALO, BATCH):
+        batch = []
+        for k in range(start, start + BATCH):
+            place = side * HALO + k
+            batch.append((blocks[k], adj[tables[3, place]], tables[4, place]))
+        add_slots(total, batch)
+
+
+def apply_low_kernel(tables, begun, low, adj, total):
     total[...] = begun[...]
-    for side, blocks in enumerate((low, high)):
-        for start in range(0, HALO, BATCH):
-            batch = []
-            for k in range(start, start + BATCH):
-                place = side * HALO + k
-                batch.append((blocks[k], adj[tables[3, place]], tables[4, place]))
-            add_slots(total, batch)
+    add_side(tables, total, low, adj, 0)
+
+
+def apply_high_kernel(tables, begun, high, adj, out, total):
+    total[...] = begun[...]
+    add_side(tables, total, high, adj, 1)
     out[...] = total[0:NBD].astype(BF16)
 
 
 def apply_halo(tables, begun, low, high, adj):
-    return pl.pallas_call(
-        apply_halo_kernel,
-        in_specs=[SMEM] + [VMEM] * 4,
+    totals = (NBD + 1, FEATS, BLK)
+    begun = pl.pallas_call(
+        apply_low_kernel,
+        in_specs=[SMEM] + [VMEM] * 3,
+        out_specs=VMEM,
+        out_shape=jax.ShapeDtypeStruct(totals, F32),
+        compiler_params=PARAMS,
+        name="apply_low",
+    )(tables, begun, low, adj)
+    return pl.pallas_call(
+        apply_high_kernel,
+        in_specs=[SMEM] + [VMEM] * 3,
         out_specs=VMEM,
         out_shape=blocks_of(),
-        scratch_shapes=[pltpu.VMEM((NBD + 1, FEATS, BLK), F32)],
-        compiler_params=PARAMS,
-        name="apply_halo",
-    )(tables, begun, low, high, adj)
+        scratch_shapes=[pltpu.VMEM(totals, F32)],
+        compiler_params=PARAMS,
+        name="apply_high",
+    )(tables, begun, high, adj)
 
 
 def apply_blocks(tables, own, sends, adj):

time: 183 us -> 184 us (level)
  waiting for transfers between devices: 4.93 us -> 1.99 us
  Pallas kernels: 16.6 us -> 18.7 us
  starting transfers between devices: 11.8 us -> 13.7 us
    ppermute x3, waiting for transfers between devices: 4.91 us -> 1.97 us  [halo(): high = lax.ppermute(send_low, NODE, backward)]
    pallas_call x3 -> x6, Pallas kernels: 3.9 us -> 6.01 us  [the longest x3 3.05 us: apply_halo(): pl.pallas_call(apply_high_kernel, in_specs=[SMEM] + [VMEM] * 3, out_specs...]
    ppermute x3, starting transfers between devices: 7.81 us -> 9.82 us  [halo(): low = lax.ppermute(send_high, NODE, forward)]
  transfers between devices with their start and end apart: 6 -> 6, of which waited for: 3 -> 3; matrix products, arithmetic and copies ran while one was open for 0% -> 0% of each run, Pallas kernels for 5% -> 6%
where the time goes in v7:
time: 184 us; the launch traced here: 183 us
  blocking collectives  146 us (79%)
  Pallas kernels  18.7 us (10%)
  starting transfers between devices  13.7 us (7%)
  waiting for transfers between devices  1.99 us (1%)
    all_to_all x9, blocking collectives, exchange(): return lax.all_to_all(array, axes, split_axis=0, concat_axis=0, tiled=True)  146 us
    ppermute x3, starting transfers between devices, halo(): low = lax.ppermute(send_high, NODE, forward)  9.82 us
    pallas_call x2, Pallas kernels, apply_own(): pl.pallas_call(apply_own_kernel, in_specs=[SMEM] + [VMEM] * 2, out_specs=...  5.8 us
    ppermute x3, starting transfers between devices, halo(): high = lax.ppermute(send_low, NODE, backward)  3.88 us
  transfers between devices with their start and end apart: 6, of which 3 were waited for; matrix products, arithmetic and copies ran while one was open for 0% of the time, Pallas kernels for 6%

profile of v7, /device:TPU:1, one launch (start us, length us, event | category | flops | bytes accessed | tf_op | source)
XLA Modules:
  0.0 183.5 jit_solution(4778725460522648904)
XLA Ops:
  1.4 0.7 add_add_fusion.slots
  2.2 0.9 copy-done.5
  3.1 0.9 split_blocks.1
  4.0 4.5 %collective-permute-start = (bf16[16,32,128]{2,1,0:T(8,128)(2,1)S(1)}, bf16[16,32,128]{2,1,0:T(8,128)(2,1)S(1)}, u32[]{:S(2)}, u32[]{:S(2)}) collective-permute-start(bf16[16,32,128]{2,1,0:T(8,128)(2,1)S(1)} %get-tuple-element.20), channel_id=1, source_target_pairs={{0,8},{8,16},{16,24},{24,32},{32,40},{40,48},{48,56},{56,64},{64,7... | collective-permute-start | bytes 393224 | tf_op jit(solution)/shard_map/ppermute | solution.py:46
  8.5 1.3 collective-permute-start.1
  9.8 2.9 %apply_own.2.begun = f32[33,32,128]{2,1,0:T(8,128)S(1)} custom-call(s32[8,128]{1,0:T(8,128)S(1)} %get-tuple-element.18.tables, bf16[32,32,128]{2,1,0:T(8,128)(2,1)S(1)} %get-tuple-element.19.own, bf16[128,128,128]{2,1,0:T(8,128)(2,1)S(1)} %copy-done), custom_call_target="tpu_custom_call" | custom-call | tf_op jit(solution)/shard_map/apply_own/pallas_call | solution.py:167
  12.8 1.0 apply_low.3.begun
  13.7 0.7 collective-permute-done.1.high
  14.4 1.0 apply_high.3
  15.4 20.9 %all_to_all.45.spread.spread_one = bf16[32,32,128]{2,1,0:T(8,128)(2,1)S(1)} all-to-all(bf16[32,32,128]{2,1,0:T(8,128)(2,1)S(1)} %apply_high.3), channel_id=1, replica_groups=mesh['x'=4,'zhi'=8,'zlo'=4,'y'=4,'core'=2] {'y','core'}, dimensions={0} | all-to-all | bytes 524288 | tf_op jit(solution)/shard_map/all_to_all | solution.py:39
  36.8 9.9 %all_to_all.46.own.blocks = bf16[32,32,128]{2,1,0:T(8,128)(2,1)S(1)} all-to-all(bf16[32,32,128]{2,1,0:T(8,128)(2,1)S(1)} %get-tuple-element.22.hidden_one), channel_id=1, replica_groups=mesh['x'=4,'zhi'=8,'zlo'=4,'y'=4,'core'=2] {'y','core'}, dimensions={0} | all-to-all | bytes 524288 | tf_op jit(solution)/shard_map/all_to_all | solution.py:39
  46.7 0.6 sends_of.1
  47.4 2.7 %collective-permute-start.2 = (bf16[16,32,128]{2,1,0:T(8,128)(2,1)S(1)}, bf16[16,32,128]{2,1,0:T(8,128)(2,1)S(1)}, u32[]{:S(2)}, u32[]{:S(2)}) collective-permute-start(bf16[16,32,128]{2,1,0:T(8,128)(2,1)S(1)} %get-tuple-element.23), channel_id=1, source_target_pairs={{0,8},{8,16},{16,24},{24,32},{32,40},{40,48},{48,56},{56,64},{64,7... | collective-permute-start | bytes 393224 | tf_op jit(solution)/shard_map/ppermute | solution.py:46
  50.0 1.3 collective-permute-start.3
  51.3 2.9 %apply_own.3.begun = f32[33,32,128]{2,1,0:T(8,128)S(1)} custom-call(s32[8,128]{1,0:T(8,128)S(1)} %get-tuple-element.18.tables, bf16[32,32,128]{2,1,0:T(8,128)(2,1)S(1)} %all_to_all.46.own.blocks, bf16[128,128,128]{2,1,0:T(8,128)(2,1)S(1)} %copy-done), custom_call_target="tpu_custom_call" | custom-call | tf_op jit(solution)/shard_map/apply_own/pallas_call | solution.py:167
  54.3 1.0 apply_low.4.begun
  55.8 1.0 apply_high.4
  56.8 11.6 %all_to_all.47.spread = bf16[32,32,128]{2,1,0:T(8,128)(2,1)S(1)} all-to-all(bf16[32,32,128]{2,1,0:T(8,128)(2,1)S(1)} %apply_high.4), channel_id=1, replica_groups=mesh['x'=4,'zhi'=8,'zlo'=4,'y'=4,'core'=2] {'y','core'}, dimensions={0} | all-to-all | bytes 524288 | tf_op jit(solution)/shard_map/all_to_all | solution.py:39
  68.7 10.0 %all_to_all.48.pre_two = bf16[32,32,128]{2,1,0:T(8,128)(2,1)S(1)} all-to-all(bf16[32,32,128]{2,1,0:T(8,128)(2,1)S(1)} %mix_two.1), channel_id=1, replica_groups=mesh['x'=4,'zhi'=8,'zlo'=4,'y'=4,'core'=2] {'y','core'}, dimensions={0} | all-to-all | bytes 524288 | tf_op jit(solution)/shard_map/all_to_all | solution.py:39
  78.7 0.8 turn.1
  79.5 2.7 %collective-permute-start.4 = (bf16[16,32,128]{2,1,0:T(8,128)(2,1)S(1)}, bf16[16,32,128]{2,1,0:T(8,128)(2,1)S(1)}, u32[]{:S(2)}, u32[]{:S(2)}) collective-permute-start(bf16[16,32,128]{2,1,0:T(8,128)(2,1)S(1)} %get-tuple-element.28), channel_id=1, source_target_pairs={{0,8},{8,16},{16,24},{24,32},{32,40},{40,48},{48,56},{56,64},{64,7... | collective-permute-start | bytes 393224 | tf_op jit(solution)/shard_map/ppermute | solution.py:46
  82.2 1.3 collective-permute-start.5
  83.5 2.6 %push_own_hidden.1 = (f32[33,32,128]{2,1,0:T(8,128)S(1)}, bf16[32,4096]{1,0:T(8,128)(2,1)}) custom-call(s32[8,128]{1,0:T(8,128)S(1)} %get-tuple-element.18.tables, bf16[32,32,128]{2,1,0:T(8,128)(2,1)S(1)} %get-tuple-element.25.own, bf16[128,128,128]{2,1,0:T(8,128)(2,1)S(1)} %copy-done, bf16[32,32,128]{2,1,0:T(8,128)(2,1)S(1)} %all_to_all.48.pre_two), custom_call_target="tpu_custom_call" | custom-call | tf_op jit(solution)/shard_map/push_own_hidden/pallas_call | solution.py:311
  86.1 1.0 apply_low.5.begun
  87.1 0.8 collective-permute-done.5.high
  87.9 1.0 apply_high.5
  88.9 11.4 %all_to_all.49.back_two = bf16[32,32,128]{2,1,0:T(8,128)(2,1)S(1)} all-to-all(bf16[32,32,128]{2,1,0:T(8,128)(2,1)S(1)} %apply_high.5), channel_id=1, replica_groups=mesh['x'=4,'zhi'=8,'zlo'=4,'y'=4,'core'=2] {'y','core'}, dimensions={0} | all-to-all | bytes 524288 | tf_op jit(solution)/shard_map/all_to_all | solution.py:39
  100.8 24.4 %all_to_all.50 = bf16[32,32,128]{2,1,0:T(8,128)(2,1)S(1)} all-to-all(bf16[32,32,128]{2,1,0:T(8,128)(2,1)S(1)} %grads.1), channel_id=1, replica_groups=mesh['x'=4,'zhi'=8,'zlo'=4,'y'=4,'core'=2] {'x','y','core'}, dimensions={0} | all-to-all | bytes 524288 | tf_op jit(solution)/shard_map/all_to_all | solution.py:39
  125.3 6.9 %all_to_all.51 = bf16[4,32,128]{2,1,0:T(8,128)(2,1)S(1)} all-to-all(bf16[4,32,128]{2,1,0:T(8,128)(2,1)S(1)} %broadcast_in_dim.12), channel_id=1, replica_groups=mesh['x'=4,'zhi'=8,'zlo'=4,'y'=4,'core'=2] {'zlo'}, dimensions={0} | all-to-all | bytes 65536 | tf_op jit(solution)/shard_map/all_to_all | solution.py:39
  132.2 36.1 %all_to_all.52 = bf16[8,32,128]{2,1,0:T(8,128)(2,1)S(1)} all-to-all(bf16[8,32,128]{2,1,0:T(8,128)(2,1)S(1)} %broadcast_in_dim.13), channel_id=1, replica_groups=mesh['x'=4,'zhi'=8,'zlo'=4,'y'=4,'core'=2] {'zhi'}, dimensions={0} | all-to-all | bytes 131072 | tf_op jit(solution)/shard_map/all_to_all | solution.py:39
  168.3 14.3 %all_to_all.53.pieces = bf16[32,32,128]{2,1,0:T(8,128)(2,1)S(1)} all-to-all(bf16[32,32,128]{2,1,0:T(8,128)(2,1)S(1)} %broadcast_in_dim.28), channel_id=1, replica_groups=mesh['x'=4,'zhi'=8,'zlo'=4,'y'=4,'core'=2] {'x','y','core'}, dimensions={0} | all-to-all | bytes 524288 | tf_op jit(solution)/shard_map/all_to_all | solution.py:39
  182.6 0.8 finish.1
  (26 shorter events, 2.0 us)
Async XLA Ops:
  2.2 0.9 copy-start.5
  3.1 6.7 %copy-start = (bf16[128,128,128]{2,1,0:T(8,128)(2,1)S(1)}, bf16[128,128,128]{2,1,0:T(8,128)(2,1)}, u32[]{:S(2)}) copy-start(bf16[128,128,128]{2,1,0:T(8,128)(2,1)} %adj.15) | copy-start | bytes 12582916
  4.0 8.7 %collective-permute-start = (bf16[16,32,128]{2,1,0:T(8,128)(2,1)S(1)}, bf16[16,32,128]{2,1,0:T(8,128)(2,1)S(1)}, u32[]{:S(2)}, u32[]{:S(2)}) collective-permute-start(bf16[16,32,128]{2,1,0:T(8,128)(2,1)S(1)} %get-tuple-element.20), channel_id=1, source_target_pairs={{0,8},{8,16},{16,24},{24,32},{32,40},{40,48},{48,56},{56,64},{64,7... | collective-permute-start | bytes 393224 | tf_op jit(solution)/shard_map/ppermute | solution.py:46
  8.5 5.9 %collective-permute-start.1 = (bf16[16,32,128]{2,1,0:T(8,128)(2,1)S(1)}, bf16[16,32,128]{2,1,0:T(8,128)(2,1)S(1)}, u32[]{:S(2)}, u32[]{:S(2)}) collective-permute-start(bf16[16,32,128]{2,1,0:T(8,128)(2,1)S(1)} %get-tuple-element.21), channel_id=1, source_target_pairs={{8,0},{16,8},{24,16},{32,24},{40,32},{48,40},{56,48},{64,56},{72,6... | collective-permute-start | bytes 393224 | tf_op jit(solution)/shard_map/ppermute | solution.py:47
  12.7 23.7 %copy-start.4 = (bf16[256,256]{1,0:T(8,128)(2,1)S(1)}, bf16[256,256]{1,0:T(8,128)(2,1)}, u32[]{:S(2)}) copy-start(bf16[256,256]{1,0:T(8,128)(2,1)} %weight.3) | copy-start | bytes 393220
  47.4 6.9 %collective-permute-start.2 = (bf16[16,32,128]{2,1,0:T(8,128)(2,1)S(1)}, bf16[16,32,128]{2,1,0:T(8,128)(2,1)S(1)}, u32[]{:S(2)}, u32[]{:S(2)}) collective-permute-start(bf16[16,32,128]{2,1,0:T(8,128)(2,1)S(1)} %get-tuple-element.23), channel_id=1, source_target_pairs={{0,8},{8,16},{16,24},{24,32},{32,40},{40,48},{48,56},{56,64},{64,7... | collective-permute-start | bytes 393224 | tf_op jit(solution)/shard_map/ppermute | solution.py:46
  50.0 5.7 %collective-permute-start.3 = (bf16[16,32,128]{2,1,0:T(8,128)(2,1)S(1)}, bf16[16,32,128]{2,1,0:T(8,128)(2,1)S(1)}, u32[]{:S(2)}, u32[]{:S(2)}) collective-permute-start(bf16[16,32,128]{2,1,0:T(8,128)(2,1)S(1)} %get-tuple-element.24), channel_id=1, source_target_pairs={{8,0},{16,8},{24,16},{32,24},{40,32},{48,40},{56,48},{64,56},{72,6... | collective-permute-start | bytes 393224 | tf_op jit(solution)/shard_map/ppermute | solution.py:47
  54.2 14.2 %copy-start.2 = (bf16[256,256]{1,0:T(8,128)(2,1)S(1)}, bf16[256,256]{1,0:T(8,128)(2,1)}, u32[]{:S(2)}) copy-start(bf16[256,256]{1,0:T(8,128)(2,1)} %weight.5) | copy-start | bytes 393220
  55.3 23.4 %copy-start.3 = (bf16[32,4096]{1,0:T(8,128)(2,1)S(1)}, bf16[32,4096]{1,0:T(8,128)(2,1)}, u32[]{:S(2)}) copy-start(bf16[32,4096]{1,0:T(8,128)(2,1)} %cotangent.1) | copy-start | bytes 786436
  56.8 29.3 %copy-start.1 = (bf16[128,128,128]{2,1,0:T(8,128)(2,1)S(1)}, bf16[128,128,128]{2,1,0:T(8,128)(2,1)}, u32[]{:S(2)}) copy-start(bf16[128,128,128]{2,1,0:T(8,128)(2,1)} %adj.17) | copy-start | bytes 12582916
  79.5 6.6 %collective-permute-start.4 = (bf16[16,32,128]{2,1,0:T(8,128)(2,1)S(1)}, bf16[16,32,128]{2,1,0:T(8,128)(2,1)S(1)}, u32[]{:S(2)}, u32[]{:S(2)}) collective-permute-start(bf16[16,32,128]{2,1,0:T(8,128)(2,1)S(1)} %get-tuple-element.28), channel_id=1, source_target_pairs={{0,8},{8,16},{16,24},{24,32},{32,40},{40,48},{48,56},{56,64},{64,7... | collective-permute-start | bytes 393224 | tf_op jit(solution)/shard_map/ppermute | solution.py:46
  82.2 5.7 %collective-permute-start.5 = (bf16[16,32,128]{2,1,0:T(8,128)(2,1)S(1)}, bf16[16,32,128]{2,1,0:T(8,128)(2,1)S(1)}, u32[]{:S(2)}, u32[]{:S(2)}) collective-permute-start(bf16[16,32,128]{2,1,0:T(8,128)(2,1)S(1)} %get-tuple-element.29), channel_id=1, source_target_pairs={{8,0},{16,8},{24,16},{32,24},{40,32},{48,40},{56,48},{64,56},{72,6... | collective-permute-start | bytes 393224 | tf_op jit(solution)/shard_map/ppermute | solution.py:47
